TPU v7x, 32 devices: a whole 2x2x4 slice. The times are simulated.
32 devices in a mesh: img: 8 (over y, x, core), ch: 4 (over z).
Axes of the slice: x: 2, y: 2, z: 4, core: 2. Of those that a mesh axis runs over, the one named last changes fastest.
Arguments:
- images: bfloat16 [64, 14, 14, 320], P('img', None, None, 'ch'), may hold values from -16 to 16
- conv_kernel: bfloat16 [2, 3, 3, 320], P(None, None, None, 'ch'), may hold values from -2 to 2
- bn_gain: bfloat16 [2, 320], P(None, 'ch'), may hold values from 0.5 to 1.5
- bn_bias: bfloat16 [2, 320], P(None, 'ch'), may hold values from -3 to 3
- mix_rows: bfloat16 [2, 14, 14], replicated, may hold values from -1.5 to 1.5
- mix_rows_bias: bfloat16 [2, 14], replicated, may hold values from -3 to 3
- mix_cols: bfloat16 [2, 14, 14], replicated, may hold values from -1.5 to 1.5
- mix_cols_bias: bfloat16 [2, 14], replicated, may hold values from -3 to 3
- join_weight: bfloat16 [2, 3, 320, 320], P(None, None, 'ch'), may hold values from -0.1875 to 0.1875
- join_bias: bfloat16 [2, 320], P(None, 'ch'), may hold values from -3 to 3
- norm_gain: bfloat16 [2, 320], P(None, 'ch'), may hold values from 0.5 to 1.5
- norm_bias: bfloat16 [2, 320], P(None, 'ch'), may hold values from -3 to 3
- weight_in: bfloat16 [2, 320, 1280], P(None, None, 'ch'), may hold values from -0.3125 to 0.3125
- bias_in: bfloat16 [2, 1280], P(None, 'ch'), may hold values from -3 to 3
- weight_out: bfloat16 [2, 1280, 320], P(None, 'ch'), may hold values from -0.15625 to 0.15625
- bias_out: bfloat16 [2, 320], P(None, 'ch'), may hold values from -3 to 3
- running_mean: float32 [2, 320], P(None, 'ch'), may hold values from -1 to 1
- running_var: float32 [2, 320], P(None, 'ch'), may hold values from 0.5 to 2
- cotangent: float32 [64, 14, 14, 320], P('img', None, None, 'ch'), may hold values from -6 to 6
Outputs:
- output: bfloat16 [64, 14, 14, 320], P('img', None, None, 'ch')
- images_grad: float32 [64, 14, 14, 320], P('img', None, None, 'ch')
- conv_kernel_grad: float32 [2, 3, 3, 320], P(None, None, None, 'ch')
- bn_gain_grad: float32 [2, 320], P(None, 'ch')
- bn_bias_grad: float32 [2, 320], P(None, 'ch')
- mix_rows_grad: float32 [2, 14, 14], replicated
- mix_rows_bias_grad: float32 [2, 14], replicated
- mix_cols_grad: float32 [2, 14, 14], replicated
- mix_cols_bias_grad: float32 [2, 14], replicated
- join_weight_grad: float32 [2, 3, 320, 320], P(None, None, 'ch')
- join_bias_grad: float32 [2, 320], P(None, 'ch')
- norm_gain_grad: float32 [2, 320], P(None, 'ch')
- norm_bias_grad: float32 [2, 320], P(None, 'ch')
- weight_in_grad: float32 [2, 320, 1280], P(None, None, 'ch')
- bias_in_grad: float32 [2, 1280], P(None, 'ch')
- weight_out_grad: float32 [2, 1280, 320], P(None, 'ch')
- bias_out_grad: float32 [2, 320], P(None, 'ch')
- running_mean_out: float32 [2, 320], P(None, 'ch')
- running_var_out: float32 [2, 320], P(None, 'ch')
All inputs are finite; a program needn't handle non-finite values.
Results may differ from a plain program's by a relative error of at most 0.024.
Values may be sent and summed in bfloat16 or wider, within the bound.
A program may use at most 128 MiB of HBM per device.

v0:
```python
import jax
import jax.numpy as jnp
from jax import lax
from jax.sharding import PartitionSpec as P

highest = lax.Precision.HIGHEST
epsilon = 1e-05


def gelu_slope(values, upstream):
    return jax.vjp(jax.nn.gelu, values)[1](upstream)[0]


def depthwise(source, kernel):
    extent = source.shape[1]
    padded = jnp.pad(source, ((0, 0), (1, 1), (1, 1), (0, 0)))
    summed = jnp.zeros_like(source)
    for offset_row in range(3):
        for offset_col in range(3):
            summed = (
                summed
                + padded[:, offset_row : offset_row + extent, offset_col : offset_col + extent, :]
                * kernel[offset_row, offset_col]
            )
    return summed


def depthwise_back(upstream, kernel, source):
    extent = source.shape[1]
    pads = ((0, 0), (1, 1), (1, 1), (0, 0))
    padded_up = jnp.pad(upstream, pads)
    padded_src = jnp.pad(source, pads)
    grad_source = jnp.zeros_like(source)
    entries = []
    for offset_row in range(3):
        for offset_col in range(3):
            grad_source = (
                grad_source
                + padded_up[
                    :,
                    2 - offset_row : 2 - offset_row + extent,
                    2 - offset_col : 2 - offset_col + extent,
                    :,
                ]
                * kernel[offset_row, offset_col]
            )
            entries.append(
                jnp.sum(
                    padded_src[
                        :, offset_row : offset_row + extent, offset_col : offset_col + extent, :
                    ]
                    * upstream,
                    axis=(0, 1, 2),
                )
            )
    return (grad_source, jnp.stack(entries).reshape(3, 3, -1))


def axial(after_conv, rows_weight, cols_weight, rows_shift, cols_shift):
    along_rows = (
        jnp.einsum("ij,bjwc->biwc", rows_weight, after_conv, precision=highest)
        + rows_shift[None, :, None, None]
    )
    along_cols = (
        jnp.einsum("ij,bhjc->bhic", cols_weight, after_conv, precision=highest)
        + cols_shift[None, None, :, None]
    )
    return (along_rows, along_cols)


def axial_back(grad_stacked, after_conv, rows_weight, cols_weight):
    grad_rows = grad_stacked[1]
    grad_cols = grad_stacked[2]
    grad_after = grad_stacked[0] + jnp.einsum(
        "ij,biwc->bjwc", rows_weight, grad_rows, precision=highest
    )
    grad_after = grad_after + jnp.einsum("ij,bhic->bhjc", cols_weight, grad_cols, precision=highest)
    grad_mix_rows = jnp.einsum("biwc,bjwc->ij", grad_rows, after_conv, precision=highest)
    grad_rows_bias = jnp.sum(grad_rows, axis=(0, 2, 3))
    grad_mix_cols = jnp.einsum("bhic,bhjc->ij", grad_cols, after_conv, precision=highest)
    grad_cols_bias = jnp.sum(grad_cols, axis=(0, 1, 3))
    return (grad_after, (grad_mix_rows, grad_rows_bias, grad_mix_cols, grad_cols_bias))


def batch_sums(first_sum, second_sum):
    return lax.psum((first_sum, second_sum), "img")


def channel_gather(values):
    return lax.all_gather(values, "ch", axis=1, tiled=True)


def channel_sum(values):
    return lax.psum_scatter(
        values.astype(jnp.bfloat16), "ch", scatter_dimension=1, tiled=True
    ).astype(jnp.float32)


def row_totals(first_sum, second_sum):
    return lax.psum((first_sum, second_sum), "ch")


def channel_forward(stacked, weights):
    join_local, in_local, out_local, join_shift, gain_local, shift_local, in_shift, out_shift = (
        weights
    )
    width_all = in_local.shape[0]
    cat_low = stacked.astype(jnp.bfloat16)
    joined_out = channel_sum(
        jnp.einsum("ktc,kcd->td", cat_low, join_local, preferred_element_type=jnp.float32)
    )
    after_join = stacked[0] + joined_out + join_shift.astype(jnp.float32)
    row_sum, row_square = row_totals(
        jnp.sum(after_join, axis=1), jnp.sum(after_join * after_join, axis=1)
    )
    row_mean = row_sum / width_all
    row_var = row_square / width_all - row_mean * row_mean
    row_inv = lax.rsqrt(row_var + epsilon)[:, None]
    centred = (after_join - row_mean[:, None]) * row_inv
    normal_low = (
        centred * gain_local.astype(jnp.float32) + shift_local.astype(jnp.float32)
    ).astype(jnp.bfloat16)
    normal_full = channel_gather(normal_low)
    hidden = jnp.dot(normal_full, in_local, preferred_element_type=jnp.float32) + in_shift.astype(
        jnp.float32
    )
    active_low = jax.nn.gelu(hidden).astype(jnp.bfloat16)
    mlp_out = channel_sum(jnp.dot(active_low, out_local, preferred_element_type=jnp.float32))
    after_mlp = after_join + mlp_out + out_shift.astype(jnp.float32)
    return (after_mlp, (cat_low, centred, row_inv, normal_full, hidden, active_low))


def channel_backward(upstream, saved, weights):
    cat_low, centred, row_inv, normal_full, hidden, active_low = saved
    join_local, in_local, out_local, join_shift, gain_local, shift_local, in_shift, out_shift = (
        weights
    )
    width_all = in_local.shape[0]
    grad_out_shift = jnp.sum(upstream, axis=0)
    upstream_full = channel_gather(upstream.astype(jnp.bfloat16))
    grad_active = jnp.einsum(
        "tc,fc->tf", upstream_full, out_local, preferred_element_type=jnp.float32
    )
    grad_out_weight = jnp.einsum(
        "tf,tc->fc", active_low, upstream_full, preferred_element_type=jnp.float32
    )
    grad_hidden = gelu_slope(hidden, grad_active).astype(jnp.bfloat16)
    grad_in_shift = jnp.sum(grad_hidden.astype(jnp.float32), axis=0)
    grad_in_weight = jnp.einsum(
        "tc,tf->cf", normal_full, grad_hidden, preferred_element_type=jnp.float32
    )
    grad_normal = channel_sum(
        jnp.einsum("tf,cf->tc", grad_hidden, in_local, preferred_element_type=jnp.float32)
    )
    grad_gain = jnp.sum(grad_normal * centred, axis=0)
    grad_shift = jnp.sum(grad_normal, axis=0)
    scaled = grad_normal * gain_local.astype(jnp.float32)
    sum_plain, sum_cross = row_totals(jnp.sum(scaled, axis=1), jnp.sum(scaled * centred, axis=1))
    grad_join = upstream + row_inv * (
        scaled - sum_plain[:, None] / width_all - centred * sum_cross[:, None] / width_all
    )
    grad_join_shift = jnp.sum(grad_join, axis=0)
    grad_joined_full = channel_gather(grad_join.astype(jnp.bfloat16))
    grad_cat = jnp.einsum(
        "td,kcd->ktc", grad_joined_full, join_local, preferred_element_type=jnp.float32
    )
    grad_join_weight = jnp.einsum(
        "ktc,td->kcd", cat_low, grad_joined_full, preferred_element_type=jnp.float32
    )
    grad_stacked = grad_cat.at[0].add(grad_join)
    return (
        grad_stacked,
        (
            grad_join_weight,
            grad_join_shift,
            grad_gain,
            grad_shift,
            grad_in_weight,
            grad_in_shift,
            grad_out_weight,
            grad_out_shift,
        ),
    )


def on_device(
    images,
    conv_kernel,
    bn_gain,
    bn_bias,
    mix_rows,
    mix_rows_bias,
    mix_cols,
    mix_cols_bias,
    join_weight,
    join_bias,
    norm_gain,
    norm_bias,
    weight_in,
    bias_in,
    weight_out,
    bias_out,
    running_mean,
    running_var,
    cotangent,
):
    layers = conv_kernel.shape[0]
    images_dev = images.shape[0]
    extent = images.shape[1]
    local_width = images.shape[3]
    tokens_dev = images_dev * extent * extent
    cell_count = images_dev * lax.axis_size("img") * extent * extent
    gathered = (
        join_weight,
        weight_in,
        weight_out,
        join_bias,
        norm_gain,
        norm_bias,
        bias_in,
        bias_out,
    )
    current = images.astype(jnp.float32)
    saved_layers = []
    chan_means = []
    chan_vars = []
    for layer_index in range(layers):
        kernel = conv_kernel[layer_index].astype(jnp.float32)
        conv_out = depthwise(current, kernel)
        sum_conv, sum_square = batch_sums(
            jnp.sum(conv_out, axis=(0, 1, 2)), jnp.sum(conv_out * conv_out, axis=(0, 1, 2))
        )
        chan_mean = sum_conv / cell_count
        chan_var = sum_square / cell_count - chan_mean * chan_mean
        inv_std = lax.rsqrt(chan_var + epsilon)
        centred = (conv_out - chan_mean) * inv_std
        normed = centred * bn_gain[layer_index].astype(jnp.float32) + bn_bias[layer_index].astype(
            jnp.float32
        )
        after_conv = current + jax.nn.gelu(normed)
        rows_weight = mix_rows[layer_index].astype(jnp.float32)
        cols_weight = mix_cols[layer_index].astype(jnp.float32)
        mix_params = (
            rows_weight,
            cols_weight,
            mix_rows_bias[layer_index].astype(jnp.float32),
            mix_cols_bias[layer_index].astype(jnp.float32),
        )
        layer_weights = tuple((item[layer_index] for item in gathered))
        along_rows, along_cols = axial(after_conv, *mix_params)
        stacked = jnp.stack([after_conv, along_rows, along_cols]).reshape(
            3, tokens_dev, local_width
        )
        after_mlp, saved_ffn = channel_forward(stacked, layer_weights)
        saved_layers.append(
            (
                current,
                kernel,
                centred,
                inv_std,
                normed,
                after_conv,
                rows_weight,
                cols_weight,
                saved_ffn,
                layer_weights,
            )
        )
        chan_means.append(chan_mean)
        chan_vars.append(chan_var)
        current = after_mlp.reshape(current.shape)
    output = current.astype(jnp.bfloat16)
    upstream = cotangent
    layer_grads = []
    for layer_index in reversed(range(layers)):
        (
            source,
            kernel,
            centred,
            inv_std,
            normed,
            after_conv,
            rows_weight,
            cols_weight,
            saved_ffn,
            layer_weights,
        ) = saved_layers[layer_index]
        rows_up = upstream.reshape(tokens_dev, local_width)
        grad_stacked, ffn_grads = channel_backward(rows_up, saved_ffn, layer_weights)
        grad_after, mix_grads = axial_back(
            grad_stacked.reshape(3, images_dev, extent, extent, local_width),
            after_conv,
            rows_weight,
            cols_weight,
        )
        grad_normed = gelu_slope(normed, grad_after)
        sum_bias, sum_gain = batch_sums(
            jnp.sum(grad_normed, axis=(0, 1, 2)), jnp.sum(grad_normed * centred, axis=(0, 1, 2))
        )
        gain_value = bn_gain[layer_index].astype(jnp.float32)
        grad_conv = (
            gain_value
            * inv_std
            * (grad_normed - sum_bias / cell_count - centred * sum_gain / cell_count)
        )
        grad_source, grad_kernel = depthwise_back(grad_conv, kernel, source)
        upstream = grad_after + grad_source
        layer_grads.append((grad_kernel, sum_gain, sum_bias) + mix_grads + ffn_grads)
    layer_grads = layer_grads[::-1]
    stacked_grads = [
        jnp.stack([grad_entry[slot_index] for grad_entry in layer_grads])
        for slot_index in range(15)
    ]
    ffn_parts = tuple(stacked_grads[7:15])
    totals = (
        lax.psum(stacked_grads[0].astype(jnp.bfloat16), "img").astype(jnp.float32),
        lax.psum(ffn_parts[0].astype(jnp.bfloat16), "img").astype(jnp.float32),
        lax.psum(ffn_parts[1].astype(jnp.bfloat16), "img").astype(jnp.float32),
        lax.psum(ffn_parts[2].astype(jnp.bfloat16), "img").astype(jnp.float32),
        lax.psum(ffn_parts[3].astype(jnp.bfloat16), "img").astype(jnp.float32),
        lax.psum(ffn_parts[4].astype(jnp.bfloat16), "img").astype(jnp.float32),
        lax.psum(ffn_parts[5].astype(jnp.bfloat16), "img").astype(jnp.float32),
        lax.psum(ffn_parts[6].astype(jnp.bfloat16), "img").astype(jnp.float32),
        lax.psum(ffn_parts[7].astype(jnp.bfloat16), "img").astype(jnp.float32),
    )
    mixing = lax.psum(
        (stacked_grads[3], stacked_grads[4], stacked_grads[5], stacked_grads[6]), ("img", "ch")
    )
    new_mean = 0.9 * running_mean + 0.1 * jnp.stack(chan_means)
    new_var = 0.9 * running_var + 0.1 * jnp.stack(chan_vars) * (cell_count / (cell_count - 1.0))
    return (
        output,
        upstream,
        totals[0],
        stacked_grads[1],
        stacked_grads[2],
        mixing[0],
        mixing[1],
        mixing[2],
        mixing[3],
        totals[1],
        totals[2],
        totals[3],
        totals[4],
        totals[5],
        totals[6],
        totals[7],
        totals[8],
        new_mean,
        new_var,
    )


def solution(mesh):
    return jax.shard_map(
        on_device,
        mesh=mesh,
        in_specs=(
            P("img", None, None, "ch"),
            P(None, None, None, "ch"),
            P(None, "ch"),
            P(None, "ch"),
            P(),
            P(),
            P(),
            P(),
            P(None, None, "ch", None),
            P(None, "ch"),
            P(None, "ch"),
            P(None, "ch"),
            P(None, None, "ch"),
            P(None, "ch"),
            P(None, "ch", None),
            P(None, "ch"),
            P(None, "ch"),
            P(None, "ch"),
            P("img", None, None, "ch"),
        ),
        out_specs=(
            P("img", None, None, "ch"),
            P("img", None, None, "ch"),
            P(None, None, None, "ch"),
            P(None, "ch"),
            P(None, "ch"),
            P(),
            P(),
            P(),
            P(),
            P(None, None, "ch", None),
            P(None, "ch"),
            P(None, "ch"),
            P(None, "ch"),
            P(None, None, "ch"),
            P(None, "ch"),
            P(None, "ch", None),
            P(None, "ch"),
            P(None, "ch"),
            P(None, "ch"),
        ),
        check_vma=False,
    )
```

profile of v0, /device:TPU:0, one launch (start us, length us, event | category | flops | bytes accessed | tf_op | source)
XLA Modules:
  0.0 643.4 jit_solution(3095719983479590005)
XLA Ops:
  16.6 15.1 %all-reduce.8 = (f32[80]{0:T(128)S(1)}, f32[80]{0:T(128)S(1)}) all-reduce(f32[80]{0:T(128)S(1)} %get-tuple-element.129, f32[80]{0:T(128)S(1)} %get-tuple-element.128), channel_id=1, replica_groups=mesh['img'=8,'ch'=4] {'img'}, use_global_device_ids=true, to_apply=%region_3.4 | all-reduce | flops 160 | bytes 1280 | tf_op jit(solution)/shard_map/psum | solution.py:86
  39.7 24.7 %reduce-scatter.7.cloned.1.call-done = bf16[1568,80]{0,1:T(8,128)(2,1)} async-done(((bf16[1568,320]{0,1:T(8,128)(2,1)}), bf16[1568,80]{0,1:T(8,128)(2,1)}) %reduce-scatter.7.cloned.1.call-update) | async-done | bytes 250896 | tf_op jit(solution)/shard_map/reduce_scatter | solution.py:94
  65.6 16.6 %all-reduce.12 = (f32[1568]{0:T(1024)S(1)}, f32[1568]{0:T(1024)S(1)}) all-reduce(f32[1568]{0:T(1024)S(1)} %get-tuple-element.137, f32[1568]{0:T(1024)S(1)} %get-tuple-element.136), channel_id=1, replica_groups=mesh['img'=8,'ch'=4] {'ch'}, use_global_device_ids=true, to_apply=%region_8.9 | all-reduce | flops 3136 | bytes 25088 | tf_op jit(solution)/shard_map/psum | solution.py:100
  82.3 19.4 %all_gather.18 = bf16[1568,320]{0,1:T(8,128)(2,1)S(1)} all-gather(bf16[1568,80]{0,1:T(8,128)(2,1)S(1)} %add_convert_fusion.2), channel_id=1, replica_groups=mesh['img'=8,'ch'=4] {'ch'}, dimensions={1}, use_global_device_ids=true | all-gather | bytes 1254400 | tf_op jit(solution)/shard_map/all_gather | solution.py:90
  104.9 2.1 convolution_convert_fusion.3
  107.7 26.1 %reduce-scatter.9.cloned.1.call-done = bf16[1568,80]{0,1:T(8,128)(2,1)} async-done(((bf16[1568,320]{0,1:T(8,128)(2,1)}), bf16[1568,80]{0,1:T(8,128)(2,1)}) %reduce-scatter.9.cloned.1.call-update) | async-done | bytes 250896 | tf_op jit(solution)/shard_map/reduce_scatter | solution.py:94
  137.6 13.9 %all-reduce.7 = (f32[80]{0:T(128)S(1)}, f32[80]{0:T(128)S(1)}) all-reduce(f32[80]{0:T(128)S(1)} %get-tuple-element.127, f32[80]{0:T(128)S(1)} %get-tuple-element.126), channel_id=1, replica_groups=mesh['img'=8,'ch'=4] {'img'}, use_global_device_ids=true, to_apply=%region_13.14 | all-reduce | flops 160 | bytes 1280 | tf_op jit(solution)/shard_map/psum | solution.py:86
  163.8 2.3 fusion.24
  170.0 2.7 fusion.1
  172.7 2.2 copy.164
  174.9 2.2 reshape.262
  180.3 33.5 %all_gather.20 = bf16[1568,320]{0,1:T(8,128)(2,1)} all-gather(bf16[1568,80]{0,1:T(8,128)(2,1)S(1)} %copy.165), channel_id=1, replica_groups=mesh['img'=8,'ch'=4] {'ch'}, dimensions={1}, use_global_device_ids=true | all-gather | bytes 1254400 | tf_op jit(solution)/shard_map/all_gather | solution.py:90
  215.0 2.2 squeeze.82
  217.3 2.2 copy.162
  219.5 2.1 fusion.158
  221.6 16.4 %all-reduce.11 = (f32[1568]{0:T(1024)S(1)}, f32[1568]{0:T(1024)S(1)}) all-reduce(f32[1568]{0:T(1024)S(1)} %get-tuple-element.135, f32[1568]{0:T(1024)S(1)} %get-tuple-element.134), channel_id=1, replica_groups=mesh['img'=8,'ch'=4] {'ch'}, use_global_device_ids=true, to_apply=%region_18.19 | all-reduce | flops 3136 | bytes 25088 | tf_op jit(solution)/shard_map/psum | solution.py:100
  239.2 19.1 %all_gather.19 = bf16[1568,320]{0,1:T(8,128)(2,1)S(1)} all-gather(bf16[1568,80]{0,1:T(8,128)(2,1)S(1)} %add_convert_fusion.1), channel_id=1, replica_groups=mesh['img'=8,'ch'=4] {'ch'}, dimensions={1}, use_global_device_ids=true | all-gather | bytes 1254400 | tf_op jit(solution)/shard_map/all_gather | solution.py:90
  264.9 3.7 convolution_convert_fusion.2
  268.7 2.2 copy.166
  274.1 3.0 fusion.29
  277.1 15.4 %reduce-scatter.15.cloned.1.call-done = bf16[1568,80]{0,1:T(8,128)(2,1)} async-done(((bf16[1568,320]{0,1:T(8,128)(2,1)}), bf16[1568,80]{0,1:T(8,128)(2,1)}) %reduce-scatter.15.cloned.1.call-update) | async-done | bytes 250896 | tf_op jit(solution)/shard_map/reduce_scatter | solution.py:94
  294.5 17.1 %all-reduce.10 = (f32[1568]{0:T(1024)S(1)}, f32[1568]{0:T(1024)S(1)}) all-reduce(f32[1568]{0:T(1024)S(1)} %get-tuple-element.133, f32[1568]{0:T(1024)S(1)} %get-tuple-element.138), channel_id=1, replica_groups=mesh['img'=8,'ch'=4] {'ch'}, use_global_device_ids=true, to_apply=%region_24.25 | all-reduce | flops 3136 | bytes 25088 | tf_op jit(solution)/shard_map/psum | solution.py:100
  311.7 9.6 %reduce-scatter.13.cloned.1.call-done = bf16[1568,80]{0,1:T(8,128)(2,1)} async-done(((bf16[1568,320]{0,1:T(8,128)(2,1)}), bf16[1568,80]{0,1:T(8,128)(2,1)}) %reduce-scatter.13.cloned.1.call-update) | async-done | bytes 250896 | tf_op jit(solution)/shard_map/reduce_scatter | solution.py:94
  321.2 3.0 fusion.164
  324.3 21.4 %all_gather.21 = bf16[1568,320]{0,1:T(8,128)(2,1)S(1)} all-gather(bf16[1568,80]{0,1:T(8,128)(2,1)S(1)} %convert_element_type.285), channel_id=1, replica_groups=mesh['img'=8,'ch'=4] {'ch'}, dimensions={1}, use_global_device_ids=true | all-gather | bytes 1254400 | tf_op jit(solution)/shard_map/all_gather | solution.py:90
  349.4 2.2 copy.167
  351.7 2.2 squeeze.88
  353.8 2.3 slice_reduce_fusion.2
  356.1 2.2 copy.172
  358.3 2.1 squeeze.90
  360.5 2.7 fusion.139
  363.2 2.2 copy.168
  365.4 2.2 squeeze.89
  367.7 5.1 fusion.155
  372.8 12.0 %all-reduce.6 = (f32[80]{0:T(128)S(1)}, f32[80]{0:T(128)S(1)}) all-reduce(f32[80]{0:T(128)S(1)} %get-tuple-element.125, f32[80]{0:T(128)S(1)} %get-tuple-element.124), channel_id=1, replica_groups=mesh['img'=8,'ch'=4] {'img'}, use_global_device_ids=true, to_apply=%region_28.29 | all-reduce | flops 160 | bytes 1280 | tf_op jit(solution)/shard_map/psum | solution.py:86
  385.4 6.5 %multiply_reduce_fusion = (bf16[80]{0:T(256)(128)(2,1)}, bf16[80]{0:T(256)(128)(2,1)}, bf16[80]{0:T(256)(128)(2,1)}, bf16[80]{0:T(256)(128)(2,1)}, bf16[80]{0:T(...) fusion(f32[8,14,14,80]{3,1,2,0:T(8,128)} %copy-done.6, ...), kind=kLoop, calls=%fused_computation.152 | loop fusion | flops 3135280 | bytes 2511840 | tf_op jit(solution)/shard_map/reduce_sum | solution.py:48
  398.1 21.4 %all_gather.22 = bf16[1568,320]{0,1:T(8,128)(2,1)S(1)} all-gather(bf16[1568,80]{0,1:T(8,128)(2,1)S(1)} %copy.176), channel_id=1, replica_groups=mesh['img'=8,'ch'=4] {'ch'}, dimensions={1}, use_global_device_ids=true | all-gather | bytes 1254400 | tf_op jit(solution)/shard_map/all_gather | solution.py:90
  419.5 4.5 fusion.173
  427.0 3.4 fusion.31
  457.2 17.7 %all-reduce.9 = (f32[1568]{0:T(1024)S(1)}, f32[1568]{0:T(1024)S(1)}) all-reduce(f32[1568]{0:T(1024)S(1)} %get-tuple-element.131, f32[1568]{0:T(1024)S(1)} %get-tuple-element.139), channel_id=1, replica_groups=mesh['img'=8,'ch'=4] {'ch'}, use_global_device_ids=true, to_apply=%region_33.34 | all-reduce | flops 3136 | bytes 25088 | tf_op jit(solution)/shard_map/psum | solution.py:100
  476.7 19.6 %all_gather.23 = bf16[1568,320]{0,1:T(8,128)(2,1)S(1)} all-gather(bf16[1568,80]{0,1:T(8,128)(2,1)S(1)} %convert_element_type.290), channel_id=1, replica_groups=mesh['img'=8,'ch'=4] {'ch'}, dimensions={1}, use_global_device_ids=true | all-gather | bytes 1254400 | tf_op jit(solution)/shard_map/all_gather | solution.py:90
  510.2 38.3 %all-reduce.4 = (f32[2,14,14]{2,1,0:T(8,128)S(1)}, f32[2,14]{1,0:T(2,128)}, f32[2,14,14]{2,1,0:T(8,128)S(1)}, f32[2,14]{1,0:T(2,128)}) all-reduce(f32[2,14,14]{2,1,0:T(8,128)S(1)} %pad_maximum_fusion.9, f32[2,14]{1,0:T(2,128)S(1)} %pad_maximum_fusion.15, ...), channel_id=1, replica_groups=mesh['img'=8,'ch'=4] {'img','ch'}, use_global_device_ids=true, to_apply=%region_57.58 | all-reduce | flops 840 | bytes 6720 | tf_op jit(solution)/shard_map/psum | solution.py:326
  549.2 4.7 fusion.154
  554.0 12.8 %all-reduce.5 = (f32[80]{0:T(128)S(1)}, f32[80]{0:T(128)S(1)}) all-reduce(f32[80]{0:T(128)S(1)} %get-tuple-element.123, f32[80]{0:T(128)S(1)} %get-tuple-element.122), channel_id=1, replica_groups=mesh['img'=8,'ch'=4] {'img'}, use_global_device_ids=true, to_apply=%region_37.38 | all-reduce | flops 160 | bytes 1280 | tf_op jit(solution)/shard_map/psum | solution.py:86
  566.8 3.1 multiply_reduce_fusion.9
  573.8 12.3 %all-reduce.13 = (bf16[2,3,3,80]{3,0,2,1:T(2,128)(2,1)S(1)}, bf16[2,80]{1,0:T(2,128)(2,1)S(1)}, bf16[2,80]{1,0:T(2,128)(2,1)S(1)}, bf16[2,80]{1,0:T(2,128)(2,1)S...) all-reduce(bf16[2,3,3,80]{3,0,2,1:T(2,128)(2,1)S(1)} %pad_maximum_f, ...), channel_id=1, replica_groups=mesh['img'=8,'ch'=4] {'img'}, use_global_device_ids=true, to_apply=%region_56.57 | all-reduce | flops 2720 | bytes 10880 | tf_op jit(solution)/shard_map/psum | solution.py:316
  591.3 39.9 %all-reduce.17.cloned.1.call-done = (bf16[2,3,80,320]{3,2,1,0:T(8,128)(2,1)}, bf16[2,320,320]{2,1,0:T(8,128)(2,1)}, bf16[2,320,320]{2,1,0:T(8,128)(2,1)}) async-done(((bf16[2,3,80,320]{3,2,1,0:T(8,128)(2,1)}, bf16[2,320,320]{2,1,0:T(8,128)(2,1)}, bf16[2,320,320]{2,1,0:T(8,128)(2,1)}), (bf16[2,3,80,320]{3,2,1,0:T(8,128)(2,1)}, bf16[2,320,320]{2,1,0:T(8,128)(2,1)}, ...) | async-done | bytes 1126416 | tf_op jit(solution)/shard_map/psum | solution.py:317
  633.1 2.0 convert_element_type.296
  (462 shorter events, 127.4 us)
Async XLA Ops:
  7.2 25.1 %copy-start.13 = (bf16[8,14,14,80]{3,0,2,1:T(8,128)(2,1)S(1)}, bf16[8,14,14,80]{3,0,2,1:T(8,128)(2,1)}, u32[]{:S(2)}) copy-start(bf16[8,14,14,80]{3,0,2,1:T(8,128)(2,1)} %param.23) | copy-start | bytes 752644
  7.2 24.5 %copy-start.60 = (bf16[2,80]{1,0:T(2,128)(2,1)S(1)}, bf16[2,80]{1,0:T(2,128)(2,1)}, u32[]{:S(2)}) copy-start(bf16[2,80]{1,0:T(2,128)(2,1)} %param.25) | copy-start | bytes 964
  7.2 57.2 %reduce-scatter.7.cloned.1.call-start = ((), (), s32[]{:S(2)}) async-start(), calls=%async_computation.6 | async-start | bytes 1331200 | tf_op jit(solution)/shard_map/reduce_scatter | solution.py:94
  10.6 21.1 %copy-start.65 = (f32[80]{0:T(128)}, f32[80]{0:T(128)S(1)}, u32[]{:S(2)}) copy-start(f32[80]{0:T(128)S(1)} %get-tuple-element.215) | copy-start | bytes 964
  10.6 22.2 %copy-start.67 = (f32[80]{0:T(128)}, f32[80]{0:T(128)S(1)}, u32[]{:S(2)}) copy-start(f32[80]{0:T(128)S(1)} %get-tuple-element.216) | copy-start | bytes 964
  10.6 22.2 %copy-start.69 = (f32[80]{0:T(128)}, f32[80]{0:T(128)S(1)}, u32[]{:S(2)}) copy-start(f32[80]{0:T(128)S(1)} %get-tuple-element.217) | copy-start | bytes 964
  10.6 22.2 %copy-start.71 = (f32[80]{0:T(128)}, f32[80]{0:T(128)S(1)}, u32[]{:S(2)}) copy-start(f32[80]{0:T(128)S(1)} %get-tuple-element.218) | copy-start | bytes 964
  10.6 22.2 %copy-start.73 = (f32[80]{0:T(128)}, f32[80]{0:T(128)S(1)}, u32[]{:S(2)}) copy-start(f32[80]{0:T(128)S(1)} %get-tuple-element.219) | copy-start | bytes 964
  10.6 22.2 %copy-start.75 = (f32[80]{0:T(128)}, f32[80]{0:T(128)S(1)}, u32[]{:S(2)}) copy-start(f32[80]{0:T(128)S(1)} %get-tuple-element.220) | copy-start | bytes 964
  10.6 22.2 %copy-start.77 = (f32[80]{0:T(128)}, f32[80]{0:T(128)S(1)}, u32[]{:S(2)}) copy-start(f32[80]{0:T(128)S(1)} %get-tuple-element.221) | copy-start | bytes 964
  10.6 22.2 %copy-start.79 = (f32[80]{0:T(128)}, f32[80]{0:T(128)S(1)}, u32[]{:S(2)}) copy-start(f32[80]{0:T(128)S(1)} %get-tuple-element.222) | copy-start | bytes 964
  10.6 22.2 %copy-start.81 = (f32[80]{0:T(128)}, f32[80]{0:T(128)S(1)}, u32[]{:S(2)}) copy-start(f32[80]{0:T(128)S(1)} %get-tuple-element.223) | copy-start | bytes 964
  12.0 21.4 %copy-start.56 = (bf16[1,14,14]{2,0,1:T(2,128)(2,1)}, bf16[1,14,14]{2,0,1:T(2,128)(2,1)S(1)}, u32[]{:S(2)}) copy-start(bf16[1,14,14]{2,0,1:T(2,128)(2,1)S(1)} %get-tuple-element.203) | copy-start | bytes 1180
  13.4 21.1 %copy-start.52 = (bf16[1,14,14]{2,0,1:T(2,128)(2,1)}, bf16[1,14,14]{2,0,1:T(2,128)(2,1)S(1)}, u32[]{:S(2)}) copy-start(bf16[1,14,14]{2,0,1:T(2,128)(2,1)S(1)} %get-tuple-element.205) | copy-start | bytes 1180
  15.4 136.7 %copy-start.121 = (f32[80]{0:T(128)}, f32[80]{0:T(128)S(1)}, u32[]{:S(2)}) copy-start(f32[80]{0:T(128)S(1)} %get-tuple-element.243) | copy-start | bytes 964
  15.4 136.7 %copy-start.123 = (f32[80]{0:T(128)}, f32[80]{0:T(128)S(1)}, u32[]{:S(2)}) copy-start(f32[80]{0:T(128)S(1)} %get-tuple-element.254) | copy-start | bytes 964
  37.4 96.4 %reduce-scatter.9.cloned.1.call-start = ((), (), s32[]{:S(2)}) async-start(), calls=%async_computation.7 | async-start | bytes 1331200 | tf_op jit(solution)/shard_map/reduce_scatter | solution.py:94
  38.1 64.7 %copy-start.21 = (bf16[2,320,320]{2,1,0:T(8,128)(2,1)S(1)}, bf16[2,320,320]{2,1,0:T(8,128)(2,1)}, u32[]{:S(2)}) copy-start(bf16[2,320,320]{2,1,0:T(8,128)(2,1)} %param.35) | copy-start | bytes 1228804
  82.1 19.6 %copy-start.48 = (f32[1568]{0:T(1024)}, f32[1568]{0:T(1024)S(1)}, u32[]{:S(2)}) copy-start(f32[1568]{0:T(1024)S(1)} %get-tuple-element.200) | copy-start | bytes 18820
  82.3 22.6 %copy-start.148 = (bf16[2,320,320]{2,1,0:T(8,128)(2,1)S(1)}, bf16[2,320,320]{2,1,0:T(8,128)(2,1)}, u32[]{:S(2)}) copy-start(bf16[2,320,320]{2,1,0:T(8,128)(2,1)} %param.37) | copy-start | bytes 1228804
  107.0 112.5 %reduce-scatter.11.cloned.1.call-start = ((), (), s32[]{:S(2)}) async-start(), calls=%async_computation.8 | async-start | bytes 1331200 | tf_op jit(solution)/shard_map/reduce_scatter | solution.py:94
  107.6 27.9 %copy-start.83 = (f32[80]{0:T(128)}, f32[80]{0:T(128)S(1)}, u32[]{:S(2)}) copy-start(f32[80]{0:T(128)S(1)} %get-tuple-element.206) | copy-start | bytes 964
  107.6 27.9 %copy-start.85 = (f32[80]{0:T(128)}, f32[80]{0:T(128)S(1)}, u32[]{:S(2)}) copy-start(f32[80]{0:T(128)S(1)} %get-tuple-element.207) | copy-start | bytes 964
  107.6 27.9 %copy-start.87 = (f32[80]{0:T(128)}, f32[80]{0:T(128)S(1)}, u32[]{:S(2)}) copy-start(f32[80]{0:T(128)S(1)} %get-tuple-element.208) | copy-start | bytes 964
  107.6 27.9 %copy-start.89 = (f32[80]{0:T(128)}, f32[80]{0:T(128)S(1)}, u32[]{:S(2)}) copy-start(f32[80]{0:T(128)S(1)} %get-tuple-element.209) | copy-start | bytes 964
  107.6 27.9 %copy-start.91 = (f32[80]{0:T(128)}, f32[80]{0:T(128)S(1)}, u32[]{:S(2)}) copy-start(f32[80]{0:T(128)S(1)} %get-tuple-element.210) | copy-start | bytes 964
  107.6 27.9 %copy-start.93 = (f32[80]{0:T(128)}, f32[80]{0:T(128)S(1)}, u32[]{:S(2)}) copy-start(f32[80]{0:T(128)S(1)} %get-tuple-element.211) | copy-start | bytes 964
  107.6 27.9 %copy-start.95 = (f32[80]{0:T(128)}, f32[80]{0:T(128)S(1)}, u32[]{:S(2)}) copy-start(f32[80]{0:T(128)S(1)} %get-tuple-element.212) | copy-start | bytes 964
  107.7 27.9 %copy-start.97 = (f32[80]{0:T(128)}, f32[80]{0:T(128)S(1)}, u32[]{:S(2)}) copy-start(f32[80]{0:T(128)S(1)} %get-tuple-element.213) | copy-start | bytes 964
  107.7 27.9 %copy-start.99 = (f32[80]{0:T(128)}, f32[80]{0:T(128)S(1)}, u32[]{:S(2)}) copy-start(f32[80]{0:T(128)S(1)} %get-tuple-element.214) | copy-start | bytes 964
  172.6 119.9 %reduce-scatter.15.cloned.1.call-start = ((), (), s32[]{:S(2)}) async-start(), calls=%async_computation.10 | async-start | bytes 1331200 | tf_op jit(solution)/shard_map/reduce_scatter | solution.py:94
  215.0 22.9 %copy-start.58 = (f32[80]{0:T(128)S(1)}, f32[80]{0:T(128)}, u32[]{:S(2)}) copy-start(f32[80]{0:T(128)} %get-tuple-element.257) | copy-start | bytes 964
  215.0 23.0 %copy-start.110 = (f32[80]{0:T(128)S(1)}, f32[80]{0:T(128)}, u32[]{:S(2)}) copy-start(f32[80]{0:T(128)} %get-tuple-element.232) | copy-start | bytes 964
  217.3 42.2 %copy-start.59 = (f32[320]{0:T(512)S(1)}, f32[320]{0:T(512)}, u32[]{:S(2)}) copy-start(f32[320]{0:T(512)} %get-tuple-element.140) | copy-start | bytes 3844
  237.9 21.5 %copy-start.22 = (bf16[2,320,320]{2,1,0:T(8,128)(2,1)S(1)}, bf16[2,320,320]{2,1,0:T(8,128)(2,1)}, u32[]{:S(2)}) copy-start(bf16[2,320,320]{2,1,0:T(8,128)(2,1)} %param.35) | copy-start | bytes 1228804
  239.2 21.0 %copy-start.26 = (bf16[1568,320]{0,1:T(8,128)(2,1)S(1)}, bf16[1568,320]{0,1:T(8,128)(2,1)}, u32[]{:S(2)}) copy-start(bf16[1568,320]{0,1:T(8,128)(2,1)} %all_gather.20) | copy-start | bytes 3010564
  239.2 21.0 %copy-start.149 = (bf16[2,320,320]{2,1,0:T(8,128)(2,1)S(1)}, bf16[2,320,320]{2,1,0:T(8,128)(2,1)}, u32[]{:S(2)}) copy-start(bf16[2,320,320]{2,1,0:T(8,128)(2,1)} %param.37) | copy-start | bytes 1228804
  264.9 56.3 %reduce-scatter.13.cloned.1.call-start = ((), (), s32[]{:S(2)}) async-start(), calls=%async_computation.9 | async-start | bytes 1331200 | tf_op jit(solution)/shard_map/reduce_scatter | solution.py:94
  268.7 186.7 %reduce-scatter.17.cloned.1.call-start = ((), (), s32[]{:S(2)}) async-start(), calls=%async_computation.11 | async-start | bytes 1331200 | tf_op jit(solution)/shard_map/reduce_scatter | solution.py:94
  271.0 50.3 %copy-start.107 = (f32[80]{0:T(128)S(1)}, f32[80]{0:T(128)}, u32[]{:S(2)}) copy-start(f32[80]{0:T(128)} %get-tuple-element.228) | copy-start | bytes 964
  321.2 25.5 %copy-start.32 = (bf16[2,3,80,320]{3,2,1,0:T(8,128)(2,1)S(1)}, bf16[2,3,80,320]{3,2,1,0:T(8,128)(2,1)}, u32[]{:S(2)}) copy-start(bf16[2,3,80,320]{3,2,1,0:T(8,128)(2,1)} %param.31) | copy-start | bytes 921604
  426.8 204.4 %all-reduce.17.cloned.1.call-start = ((), (), s32[]{:S(2)}) async-start(), calls=%async_computation.12 | async-start | bytes 2703360 | tf_op jit(solution)/shard_map/psum | solution.py:317
  454.0 20.8 %copy-start.19 = (f32[1568,80]{0,1:T(8,128)S(1)}, f32[1568,80]{0,1:T(8,128)}, u32[]{:S(2)}) copy-start(f32[1568,80]{0,1:T(8,128)} %copy.177) | copy-start | bytes 1505284
  457.2 39.1 %copy-start.36 = (bf16[1,1568,80]{1,2,0:T(8,128)(2,1)S(1)}, bf16[1,1568,80]{1,2,0:T(8,128)(2,1)}, u32[]{:S(2)}) copy-start(bf16[1,1568,80]{1,2,0:T(8,128)(2,1)} %copy-done.35) | copy-start | bytes 752644
  457.2 39.1 %copy-start.38 = (bf16[1,1568,80]{1,2,0:T(8,128)(2,1)S(1)}, bf16[1,1568,80]{1,2,0:T(8,128)(2,1)}, u32[]{:S(2)}) copy-start(bf16[1,1568,80]{1,2,0:T(8,128)(2,1)} %copy-done.37) | copy-start | bytes 752644
  457.2 39.1 %copy-start.40 = (bf16[1,1568,80]{1,2,0:T(8,128)(2,1)S(1)}, bf16[1,1568,80]{1,2,0:T(8,128)(2,1)}, u32[]{:S(2)}) copy-start(bf16[1,1568,80]{1,2,0:T(8,128)(2,1)} %copy-done.39) | copy-start | bytes 752644
  476.7 20.9 %copy-start.33 = (bf16[2,3,80,320]{3,2,1,0:T(8,128)(2,1)S(1)}, bf16[2,3,80,320]{3,2,1,0:T(8,128)(2,1)}, u32[]{:S(2)}) copy-start(bf16[2,3,80,320]{3,2,1,0:T(8,128)(2,1)} %param.31) | copy-start | bytes 921604
  506.0 43.2 %copy-start.5 = (f32[8,14,14,80]{3,1,2,0:T(8,128)S(1)}, f32[8,14,14,80]{3,1,2,0:T(8,128)}, u32[]{:S(2)}) copy-start(f32[8,14,14,80]{3,1,2,0:T(8,128)} %copy-done.4) | copy-start | bytes 1505284
  (109 other events, 758.2 us)
Sparse Core Ops, SparseCore 0:
  37.5 26.9 reduce-scatter.6
  107.1 26.5 reduce-scatter.8
  172.8 36.6 reduce-scatter.10
  265.0 27.4 reduce-scatter.14
  294.7 26.5 reduce-scatter.12
  426.9 26.1 reduce-scatter.16
  573.7 57.3 all-reduce.16
where the time goes:
time: 653 us; the launch traced here: 643 us
  blocking collectives  307 us (47%)
  waiting for transfers between devices  116 us (18%)
  other arithmetic  72.5 us (11%)
  local copies, waits for them, and re-layouts  71.1 us (11%)
  matrix products  60.6 us (9%)
  between operations  16.3 us (2%)
    all_gather x6, blocking collectives, channel_gather(): return lax.all_gather(values, 'ch', axis=1, tiled=True)  134 us
    reduce_scatter x6, waiting for transfers between devices, channel_sum(): lax.psum_scatter(values.astype(jnp.bfloat16), 'ch', scatter_dimension=1,...  75.8 us
    psum x4, blocking collectives, row_totals(): return lax.psum((first_sum, second_sum), 'ch')  67.8 us
    psum x4, blocking collectives, batch_sums(): return lax.psum((first_sum, second_sum), 'img')  53.8 us
    psum x1, waiting for transfers between devices, on_device(): lax.psum(ffn_parts[0].astype(jnp.bfloat16), 'img').astype(jnp.float32)  39.9 us
    psum x1, blocking collectives, on_device(): lax.psum((stacked_grads[3], stacked_grads[4], stacked_grads[5], stacked_g...  38.3 us
    unnamed x306, local copies, waits for them, and re-layouts  15.7 us
  transfers between devices with their start and end apart: 7, of which 5 were waited for; matrix products, arithmetic and copies ran while one was open for 10% of the time, Pallas kernels for 0%

commit v1 on v0

v1 whole, which is shorter than its diff:
```python
import functools
from types import SimpleNamespace

import jax
import jax.numpy as jnp
from jax import lax
from jax.experimental import pallas as pl
from jax.experimental.pallas import tpu as pltpu
from jax.sharding import PartitionSpec as P

f32 = jnp.float32
bf16 = jnp.bfloat16
MESH = pl.DeviceIdType.MESH
epsilon = 1e-05
LANES = 128
ROOT = 0.7978845608028654
CUBE = 0.044715


def up(number, step):
    return -(-number // step) * step


def dot_nn(left, right):
    return lax.dot_general(left, right, (((1,), (0,)), ((), ())), preferred_element_type=f32)


def dot_nt(left, right):
    return lax.dot_general(left, right, (((1,), (1,)), ((), ())), preferred_element_type=f32)


def dot_tn(left, right):
    return lax.dot_general(left, right, (((0,), (0,)), ((), ())), preferred_element_type=f32)


def gelu_both(value):
    square = value * value
    bend = jnp.tanh(value * (ROOT + (ROOT * CUBE) * square))
    half = 0.5 + 0.5 * bend
    slope = half + (0.5 * value) * (1.0 - bend * bend) * (ROOT + (3.0 * ROOT * CUBE) * square)
    return value * half, slope


def lane_index(shape):
    return lax.broadcasted_iota(jnp.int32, shape, len(shape) - 1)


def assemble(pieces, tiles):
    placed = [None] * tiles
    axis = pieces[0][0].ndim - 1
    lane = lane_index(pieces[0][0].shape)

    def add(place, value):
        placed[place] = value if placed[place] is None else placed[place] + value

    for tile, offset, width in pieces:
        first, shift = divmod(offset, LANES)
        if shift == 0:
            add(first, tile)
            continue
        turned = pltpu.roll(tile, shift, axis)
        if shift + width <= LANES:
            add(first, turned)
        else:
            add(first, jnp.where(lane >= shift, turned, 0.0))
            add(first + 1, jnp.where(lane < shift, turned, 0.0))
    return [jnp.zeros(pieces[0][0].shape, f32) if tile is None else tile for tile in placed]


def cut(tiles, offset, width):
    axis = tiles[0].ndim - 1
    lane = lane_index(tiles[0].shape)
    first, shift = divmod(offset, LANES)
    if shift == 0:
        value = tiles[first]
    else:
        value = pltpu.roll(tiles[first], LANES - shift, axis)
        if shift + width > LANES:
            value = jnp.where(lane < LANES - shift, value, pltpu.roll(tiles[first + 1], LANES - shift, axis))
    return value if width == LANES else jnp.where(lane < width, value, 0.0)


class Sizes:
    def __init__(self, ni, nk, images, conv_kernel, weight_in):
        self.ni, self.nk, self.nd = ni, nk, ni * nk
        self.chips = ni // 2
        self.group, self.high, self.wide, self.cl = images.shape
        self.layers = conv_kernel.shape[0]
        self.own = self.group // nk
        self.channels = weight_in.shape[1]
        self.fl = weight_in.shape[2]
        self.tj = up(self.wide, 16)
        self.cp = up(self.channels, LANES)
        self.ct = self.cp // LANES
        self.bh = self.own * self.high
        self.rows = self.bh * self.tj
        self.rb = self.high * self.tj
        self.cells = ni * self.group * self.high * self.wide
        self.clp = up(self.cl, 16)
        def part_rows(rows):
            return up(-(-rows // ni), 16)

        join_rows, mlp_rows = 3 * self.clp, 2 * self.fl
        apart, together = part_rows(join_rows) + part_rows(mlp_rows), part_rows(join_rows + mlp_rows)
        if 4 * apart <= 5 * together:
            self.parts = {"m": part_rows(mlp_rows), "j": part_rows(join_rows)}
            self.join_kind, self.join_row = "j", 0
        else:
            self.parts = {"m": together}
            self.join_kind, self.join_row = "m", mlp_rows
        self.kg = next((n for n in range(1, nk + 1) if nk % n == 0 and n * self.fl % LANES == 0), nk)
        self.nkg = nk // self.kg
        self.ft = self.kg * self.fl
        self.ftiles = -(-self.fl // LANES)
        self.step = next(n for n in (4, 2, 1) if self.bh % n == 0)
        self.lines = next(n for n in (7, 4, 2, 1) if self.high % n == 0)
        self.stat = up(2 * self.ct, 8)


PARAM_ROWS = 16
SMALL_ROWS = 40


def scratch_list(z):
    tile = (z.own, z.high, z.tj, LANES)
    layer, rows, cp = z.layers, z.rows, z.cp
    shapes = dict(
        xl=((z.group, z.high + 2, z.tj, LANES), f32),
        al=((z.group, z.high, z.tj, LANES), f32),
        stage=((4, z.nk) + tile, bf16),
        land=((4, z.nk) + tile, bf16),
        par=((layer, PARAM_ROWS + 8, LANES), f32),
        pars=((z.nk, layer, PARAM_ROWS + 8, LANES), f32),
        pf=((layer, PARAM_ROWS, cp), f32),
        bi=((layer, z.nkg, 8, z.ft), f32),
        msg=((2 * layer, z.stat, LANES), f32),
        stats=((2 * layer, z.nd, z.stat, LANES), f32),
        jf=((layer, 3, cp, cp), bf16),
        mix=((layer, 4, z.rb, z.rb), bf16),
        mixb=((layer, 2, z.rb, 8), f32),
        mixs=((4, 16, 16), f32),
        x=((layer, z.own, z.high + 2, z.tj, cp), f32),
        a=((layer, z.bh, z.tj, cp), f32),
        sz=((layer, z.bh, z.tj, cp), f32),
        mv=((layer, 8, cp), f32),
        u=((z.bh, z.tj, cp), f32),
        cat=((layer, 3, z.own, z.rb, cp), bf16),
        w=((z.bh, z.tj, cp), f32),
        what=((layer, z.bh, z.tj, cp), f32),
        inv=((layer, z.bh, z.tj, LANES), f32),
        yb=((layer, z.bh, z.tj, cp), bf16),
        hs=((layer, z.nkg, z.own, z.rb, z.ft), f32),
        gb=((layer, z.nkg, z.own, z.rb, z.ft), bf16),
        gh=((z.own, z.rb, z.ft), bf16),
        o=((z.bh, z.tj, cp), f32),
        gx=((z.bh, z.tj, cp), f32),
        gob=((z.bh, z.tj, cp), bf16),
        gw=((z.bh, z.tj, cp), f32),
        gsb=((z.bh, z.tj, cp), bf16),
        gpq=((2, z.own, z.rb, cp), bf16),
        gu=((z.bh, z.tj, cp), f32),
        gz=((z.bh, z.tj, cp), f32),
        ga=((z.own, z.high + 2, z.tj, cp), f32),
        sg=((PARAM_ROWS, cp), f32),
        bg=((8, z.nkg * z.ft), f32),
        mg=((16, LANES), f32),
        sgm=((layer, z.nk, 32, LANES), f32),
        sgk=((layer, z.nk, 32, LANES), f32),
        sgz=((layer, 32, LANES), f32),
        sgi=((layer, z.ni, 32, LANES), f32),
    )
    groups = []
    for part in z.parts.values():
        whole_rows = z.ni * part
        groups.append(
            dict(
                wt=((layer, z.nk, whole_rows, cp), bf16),
                gr=((layer, z.nk, whole_rows, cp), bf16),
                r1=((layer, z.chips, z.nk, part, cp), bf16),
                r2=((layer, z.chips - 1, z.nk, part, cp), bf16),
                r3=((layer, z.nk - 1, part, cp), bf16),
                fin=((layer, whole_rows, cp), bf16),
            )
        )
    return shapes, groups


def whole(z, *refs):
    inputs, refs = refs[:17], refs[17:]
    outputs, refs = refs[: 3 + len(z.parts)], refs[3 + len(z.parts) :]
    shapes, groups = scratch_list(z)
    r = SimpleNamespace(**dict(zip(shapes, refs[: len(shapes)], strict=True)))
    (r.images, r.conv_kernel, r.bn_gain, r.bn_bias, r.mix_rows, r.mix_rows_bias, r.mix_cols, r.mix_cols_bias) = inputs[:8]
    (r.join_weight, r.join_bias, r.norm_gain, r.norm_bias, r.weight_in, r.bias_in, r.weight_out, r.bias_out) = inputs[8:16]
    r.cotangent = inputs[16]
    r.out_y, r.out_g, r.out_s = outputs[:3]
    r.outs = dict(zip(z.parts, outputs[3:], strict=True))
    refs = refs[len(shapes) :]
    table = SimpleNamespace(**{name: {} for name in groups[0]})
    for kind, group in zip(z.parts, groups, strict=True):
        for name, ref in zip(group, refs[: len(group)], strict=True):
            getattr(table, name)[kind] = ref
        refs = refs[len(group) :]
    r.wt, r.gr, r.r1, r.r2, r.r3, r.fin = table.wt, table.gr, table.r1, table.r2, table.r3, table.fin
    ssem, rsem = refs
    ni, nk, nd, layers = z.ni, z.nk, z.nd, z.layers
    i = lax.axis_index("img")
    k = lax.axis_index("ch")
    core = lax.rem(i, 2)
    chip = lax.div(i, 2)
    partner = i + 1 - 2 * core
    events = {}
    sends = []

    def at(image_index, channel_index):
        return {"img": image_index, "ch": channel_index}

    def event(name):
        return events.setdefault(name, len(events))

    def send(name, src, dst, device):
        number = event(name)
        pltpu.make_async_remote_copy(
            src_ref=src,
            dst_ref=dst,
            send_sem=ssem.at[number],
            recv_sem=rsem.at[number],
            device_id=device,
            device_id_type=MESH,
        ).start()

    def arrived(name, ref):
        number = event(name)
        sends.append((number, ref))
        pltpu.make_async_remote_copy(
            src_ref=ref,
            dst_ref=ref,
            send_sem=ssem.at[number],
            recv_sem=rsem.at[number],
            device_id=at(partner, k),
            device_id_type=MESH,
        ).wait_recv()

    def loop(count, body, start=0):
        def run(index, carry):
            body(index)
            return carry

        lax.fori_loop(start, count, run, 0)

    barrier = pltpu.get_barrier_semaphore()

    def greet(j):
        pl.semaphore_signal(
            barrier,
            inc=1,
            device_id=at(lax.rem(i + lax.div(j, nk), ni), lax.rem(k + lax.rem(j, nk), nk)),
            device_id_type=MESH,
        )

    loop(nd, greet, 1)

    def exchange_start(slot):
        stats, msg = r.stats, r.msg
        mine = i * nk + k
        stats[slot, mine] = msg[slot]

        def one(j):
            send(
                ("st", slot),
                msg.at[slot],
                stats.at[slot, mine],
                at(lax.rem(i + lax.div(j, nk), ni), lax.rem(k + lax.rem(j, nk), nk)),
            )

        loop(nd, one, 1)

    def exchange_wait(slot):
        arrived(("st", slot), r.stats.at[slot, pl.ds(0, nd - 1)])

    def swap_start(slot):
        for step in range(1, nk):
            other = lax.rem(k + step, nk)
            send(("sw", slot), r.stage.at[slot, other], r.land.at[slot, k], at(i, other))

    def swap_wait(slot):
        arrived(("sw", slot), r.land.at[slot, pl.ds(0, nk - 1)])

    def own_tile(slot):
        r.land[slot, k] = r.stage[slot, k]

    def rps(kind):
        return z.parts[kind]

    def piece(number, size):
        return pl.ds(pl.multiple_of(number * size, 16), size)

    done = set()

    def once(work):
        def run(layer, kind):
            if kind in z.parts and (work, layer, kind) not in done:
                done.add((work, layer, kind))
                work(layer, kind)

        return run

    @once
    def weights_along(layer, kind):
        buffer = r.wt[kind]
        place = piece(i, rps(kind))
        for step in range(1, nk):
            ref = buffer.at[layer, k, place]
            send(("w1", layer, kind), ref, ref, at(i, lax.rem(k + step, nk)))

    @once
    def weights_across(layer, kind):
        buffer = r.wt[kind]
        size = rps(kind)
        arrived(("w1", layer, kind), buffer.at[layer, pl.ds(0, nk - 1), pl.ds(0, size)])
        for step in range(1, nk):
            ref = buffer.at[layer, lax.rem(k + step, nk), piece(i, size)]
            for turn in range(1, z.chips):
                send(("w2", layer, kind), ref, ref, at(2 * lax.rem(chip + turn, z.chips) + core, k))

    @once
    def weights_pair(layer, kind):
        buffer = r.wt[kind]
        size = rps(kind)
        arrived(("w2", layer, kind), buffer.at[layer, pl.ds(0, nk - 1), pl.ds(0, (z.chips - 1) * size)])
        for step in range(1, nk):
            for other in range(z.chips):
                ref = buffer.at[layer, lax.rem(k + step, nk), piece(2 * other + core, size)]
                send(("w3", layer, kind), ref, ref, at(partner, k))

    @once
    def weights_ready(layer, kind):
        size = rps(kind)
        arrived(("w3", layer, kind), r.wt[kind].at[layer, pl.ds(0, nk - 1), pl.ds(0, z.chips * size)])
        if kind == z.join_kind:
            for branch in range(3):
                row = z.join_row + branch * z.clp
                parts = [
                    r.wt[kind][layer, part, row : row + z.cl, :].astype(f32)
                    for part in range(nk)
                ]
                if z.cp > z.channels:
                    parts.append(jnp.zeros((z.cp - z.channels, z.cp), f32))
                r.jf[layer, branch] = jnp.concatenate(parts, axis=0).astype(bf16)

    @once
    def reduce_pair(layer, kind):
        size = rps(kind)
        for other in range(z.chips):
            send(
                ("r1", layer, kind),
                r.gr[kind].at[layer, :, piece(2 * other + 1 - core, size)],
                r.r1[kind].at[layer, other],
                at(partner, k),
            )

    @once
    def reduce_across(layer, kind):
        size = rps(kind)
        arrived(("r1", layer, kind), r.r1[kind].at[layer])
        for other in range(z.chips):
            place = piece(2 * other + core, size)

            def add(part, other=other, place=place):
                r.gr[kind][layer, part, place] = (
                    r.gr[kind][layer, part, place].astype(f32) + r.r1[kind][layer, other, part].astype(f32)
                ).astype(bf16)

            loop(nk, add)
        for turn in range(1, z.chips):
            other = lax.rem(chip + turn, z.chips)
            send(
                ("r2", layer, kind),
                r.gr[kind].at[layer, :, piece(2 * other + core, size)],
                r.r2[kind].at[layer, turn - 1],
                at(2 * other + core, k),
            )

    @once
    def reduce_along(layer, kind):
        arrived(("r2", layer, kind), r.r2[kind].at[layer])
        place = piece(i, rps(kind))

        def add(part):
            total = r.gr[kind][layer, part, place].astype(f32)
            for turn in range(z.chips - 1):
                total = total + r.r2[kind][layer, turn, part].astype(f32)
            r.gr[kind][layer, part, place] = total.astype(bf16)

        loop(nk, add)
        for step in range(1, nk):
            other = lax.rem(k + step, nk)
            send(
                ("r3", layer, kind),
                r.gr[kind].at[layer, other, place],
                r.r3[kind].at[layer, step - 1],
                at(i, other),
            )

    @once
    def spread_across(layer, kind):
        size = rps(kind)
        arrived(("r3", layer, kind), r.r3[kind].at[layer])
        place = piece(i, size)
        total = r.gr[kind][layer, k, place].astype(f32)
        for step in range(nk - 1):
            total = total + r.r3[kind][layer, step].astype(f32)
        r.fin[kind][layer, place] = total.astype(bf16)
        ref = r.fin[kind].at[layer, place]
        for turn in range(1, z.chips):
            send(("r4", layer, kind), ref, ref, at(2 * lax.rem(chip + turn, z.chips) + core, k))

    @once
    def spread_pair(layer, kind):
        size = rps(kind)
        arrived(("r4", layer, kind), r.fin[kind].at[layer, pl.ds(0, (z.chips - 1) * size)])
        for other in range(z.chips):
            ref = r.fin[kind].at[layer, piece(2 * other + core, size)]
            send(("r5", layer, kind), ref, ref, at(partner, k))

    @once
    def spread_ready(layer, kind):
        arrived(("r5", layer, kind), r.fin[kind].at[layer, pl.ds(0, z.chips * rps(kind))])
        r.outs[kind][layer] = r.fin[kind][layer]

    cleared = [r.xl, r.x, r.ga, r.par, r.pf, r.bi, r.mixs, r.mg, r.sg, r.bg, r.sgm]
    for ref in cleared + list(r.gr.values()):
        if len(ref.shape) > 3:

            def clear(index, ref=ref):
                ref[index] = jnp.zeros(ref.shape[1:], ref.dtype)

            loop(ref.shape[0], clear)
        else:
            ref[...] = jnp.zeros(ref.shape, ref.dtype)

    tile_row = lax.broadcasted_iota(jnp.int32, (z.tj, LANES), 0)
    inside = tile_row < z.wide

    def take_image(n):
        def line(h):
            r.xl[n, h + 1, 0 : z.wide, 0 : z.cl] = r.images[n, h].astype(f32)

        loop(z.high, line)
        r.stage[0, lax.div(n, z.own), lax.rem(n, z.own)] = r.xl[n, 1 : z.high + 1].astype(bf16)

    loop(z.group, take_image)

    small = [
        (9, r.bn_gain),
        (10, r.bn_bias),
        (11, r.join_bias),
        (12, r.norm_gain),
        (13, r.norm_bias),
        (14, r.bias_out),
    ]
    for row, ref in small:
        values = ref[...].astype(f32)
        for layer in range(layers):
            r.par[layer, row : row + 1, 0 : z.cl] = values[layer : layer + 1]
    values = r.bias_in[...].astype(f32)
    for layer in range(layers):
        for tap in range(3):
            r.par[layer, 3 * tap : 3 * tap + 3, 0 : z.cl] = r.conv_kernel[layer, tap].astype(f32)
        for tile in range(z.ftiles):
            stop = min(z.fl, LANES * (tile + 1))
            r.par[layer, PARAM_ROWS + tile : PARAM_ROWS + tile + 1, 0 : stop - LANES * tile] = values[
                layer : layer + 1, LANES * tile : stop
            ]

    def conv(lines, taps):
        count = lines.shape[0] - 2
        shifted = (pltpu.roll(lines, 1, 1), lines, pltpu.roll(lines, z.tj - 1, 1))
        total = None
        for down in range(3):
            for side in range(3):
                term = shifted[side][down : down + count] * taps[3 * down + side]
                total = term if total is None else total + term
        return total

    taps = [r.par[0, t : t + 1, :] for t in range(9)]

    def conv_local(n, carry):
        value = jnp.where(inside, conv(r.xl[n], taps), 0.0)
        r.al[n] = value
        return carry + jnp.sum(value, axis=0)

    local_cells = z.group * z.high * z.wide
    total = lax.fori_loop(0, z.group, conv_local, jnp.zeros((z.tj, LANES), f32))
    local_mean = jnp.sum(total, axis=0, keepdims=True) * (1.0 / local_cells)

    def square_local(n, carry):
        away = jnp.where(inside, r.al[n] - local_mean, 0.0)
        return carry + jnp.sum(away * away, axis=0)

    total = lax.fori_loop(0, z.group, square_local, jnp.zeros((z.tj, LANES), f32))
    local_var = jnp.sum(total, axis=0, keepdims=True) * (1.0 / local_cells)
    r.msg[0] = jnp.concatenate([local_mean, local_var, jnp.zeros((z.stat - 2, LANES), f32)], axis=0)

    pl.semaphore_wait(barrier, nd - 1)

    swap_start(0)
    exchange_start(0)
    r.pars[k] = r.par[...]
    for step in range(1, nk):
        send("par", r.par, r.pars.at[k], at(i, lax.rem(k + step, nk)))
    own_tile(0)

    blank = jnp.zeros((z.cl, z.cp - z.channels), f32)
    blank_hidden = jnp.zeros((z.fl, z.cp - z.channels), f32)
    for layer in range(layers):
        for kind in z.parts:
            r.wt[kind][layer, k] = jnp.zeros(r.wt[kind].shape[2:], bf16)
        for branch in range(3):
            value = r.join_weight[layer, branch].astype(f32)
            if z.cp > z.channels:
                value = jnp.concatenate([value, blank], axis=1)
            row = z.join_row + branch * z.clp
            r.wt[z.join_kind][layer, k, row : row + z.cl, :] = value.astype(bf16)
        for place, value in (
            (0, r.weight_in[layer].astype(f32).T),
            (z.fl, r.weight_out[layer].astype(f32)),
        ):
            if z.cp > z.channels:
                value = jnp.concatenate([value, blank_hidden], axis=1)
            r.wt["m"][layer, k, place : place + z.fl, :] = value.astype(bf16)
        if layer == 0:
            for kind in ("j", "m"):
                weights_along(0, kind)

    select_row = lax.broadcasted_iota(jnp.int32, (z.rb, 16), 0)
    select_col = lax.broadcasted_iota(jnp.int32, (z.rb, 16), 1)
    pick_high = (lax.div(select_row, z.tj) == select_col).astype(f32)
    pick_wide = (lax.rem(select_row, z.tj) == select_col).astype(f32)
    low_high, low_wide = pick_high.astype(bf16), pick_wide.astype(bf16)
    full_row = lax.broadcasted_iota(jnp.int32, (z.rb, z.rb), 0)
    full_col = lax.broadcasted_iota(jnp.int32, (z.rb, z.rb), 1)
    same_wide = (lax.rem(full_row, z.tj) == lax.rem(full_col, z.tj)) & (lax.rem(full_row, z.tj) < z.wide)
    same_high = lax.div(full_row, z.tj) == lax.div(full_col, z.tj)
    for layer in range(layers):
        for which, (maps, shifts, pick, same, extent) in enumerate(
            (
                (r.mix_rows, r.mix_rows_bias, low_high, same_wide, z.high),
                (r.mix_cols, r.mix_cols_bias, low_wide, same_high, z.wide),
            )
        ):
            r.mixs[which, 0:extent, 0:extent] = maps[layer].astype(f32)
            table = r.mixs[which].astype(bf16)
            for turned, half in ((0, dot_nn(pick, table)), (1, dot_nt(pick, table))):
                spread = dot_nt(half.astype(bf16), pick)
                r.mix[layer, 2 * which + turned] = jnp.where(same, spread, 0.0).astype(bf16)
            r.mixs[2 + which, 0:1, 0:extent] = shifts[layer : layer + 1, :].astype(f32)
            r.mixb[layer, which] = dot_nt(pick, r.mixs[2 + which, 0:8, :].astype(bf16))

    exchange_wait(0)
    arrived("par", r.pars.at[pl.ds(0, nk - 1)])
    for layer in range(layers):
        tiles = assemble(
            [(r.pars[part, layer, 0:PARAM_ROWS, :], part * z.cl, z.cl) for part in range(nk)], z.ct
        )
        for tile in range(z.ct):
            r.pf[layer, :, LANES * tile : LANES * (tile + 1)] = tiles[tile]
        for block in range(z.nkg):
            pieces = []
            for part in range(z.kg):
                for tile in range(z.ftiles):
                    row = PARAM_ROWS + tile
                    value = r.pars[block * z.kg + part, layer, row : row + 1, :]
                    width = min(LANES, z.fl - LANES * tile)
                    pieces.append((jnp.broadcast_to(value, (8, LANES)), part * z.fl + LANES * tile, width))
            tiles = assemble(pieces, -(-z.ft // LANES))
            for tile, value in enumerate(tiles):
                stop = min(z.ft, LANES * (tile + 1))
                r.bi[layer, block, :, LANES * tile : stop] = value[:, 0 : stop - LANES * tile]

    def param(layer, row):
        return r.pf[layer, row : row + 1, :]

    def wide_row(tiles):
        return jnp.concatenate(tiles, axis=1)

    def combine(means, variances):
        count = means.shape[0]
        mean = jnp.sum(means, axis=0, keepdims=True) * (1.0 / count)
        away = means - mean
        var = jnp.sum(variances + away * away, axis=0, keepdims=True) * (1.0 / count)
        return mean[0], var[0]

    lane_full = lane_index((z.step, z.tj, z.cp))
    column_full = lax.broadcasted_iota(jnp.int32, (z.step, z.tj, z.cp), 1)
    real_lane = lane_full < z.channels
    real_column = column_full < z.wide
    blocks = z.bh // z.step

    def place_of(t):
        return lax.div(t, z.high), lax.rem(t, z.high)

    def unpack(slot, store):
        def image(b):
            def lines(part):
                start = part * z.lines
                tiles = assemble(
                    [
                        (r.land[slot, source, b, pl.ds(start, z.lines)].astype(f32), source * z.cl, z.cl)
                        for source in range(nk)
                    ],
                    z.ct,
                )
                store(b, start, tiles)

            loop(z.high // z.lines, lines)

        loop(z.own, image)

    def store_x(b, start, tiles):
        for tile in range(z.ct):
            r.x[0, b, pl.ds(start + 1, z.lines), :, LANES * tile : LANES * (tile + 1)] = tiles[tile]

    def store_gx(b, start, tiles):
        for tile in range(z.ct):
            r.gx[pl.ds(b * z.high + start, z.lines), :, LANES * tile : LANES * (tile + 1)] = tiles[tile]

    def pack(slot, take):
        def image(b):
            def lines(part):
                start = part * z.lines
                tiles = [take(b, start, tile) for tile in range(z.ct)]
                for target in range(nk):
                    r.stage[slot, target, b, pl.ds(start, z.lines)] = cut(tiles, target * z.cl, z.cl).astype(bf16)

            loop(z.high // z.lines, lines)

        loop(z.own, image)

    swap_wait(0)
    unpack(0, store_x)

    own_cells = z.own * z.high * z.wide

    for layer in range(layers):

        def conv_part(t, carry, layer=layer):
            b, part = lax.div(t, z.high // z.lines), lax.rem(t, z.high // z.lines)
            start = part * z.lines
            sums = []
            for tile in range(z.ct):
                lanes = slice(LANES * tile, LANES * (tile + 1))
                taps = [r.pf[layer, row : row + 1, lanes] for row in range(9)]
                value = conv(r.x[layer, b, pl.ds(start, z.lines + 2), :, lanes], taps)
                value = jnp.where(inside, value, 0.0)
                r.a[layer, pl.ds(b * z.high + start, z.lines), :, lanes] = value
                sums.append(carry[tile] + jnp.sum(value, axis=0))
            return tuple(sums)

        sums = lax.fori_loop(
            0,
            z.own * (z.high // z.lines),
            conv_part,
            tuple(jnp.zeros((z.tj, LANES), f32) for _ in range(z.ct)),
        )
        if layer == 0:
            stats = r.stats[0].reshape(ni, nk, z.stat, LANES)
            whole_mean, whole_var = [], []
            for part in range(nk):
                mean, var = combine(stats[:, part, 0:1, :], stats[:, part, 1:2, :])
                whole_mean.append((jnp.broadcast_to(mean, (8, LANES)), part * z.cl, z.cl))
                whole_var.append((jnp.broadcast_to(var, (8, LANES)), part * z.cl, z.cl))
            mean = wide_row([tile[0:1] for tile in assemble(whole_mean, z.ct)])
            var = wide_row([tile[0:1] for tile in assemble(whole_var, z.ct)])
        else:
            own_mean = wide_row([jnp.sum(tile, axis=0, keepdims=True) for tile in sums]) * (1.0 / own_cells)

            def square_part(t, carry, layer=layer, own_mean=own_mean):
                value = r.a[layer, pl.ds(t * z.step, z.step)] - own_mean
                value = jnp.where(real_column, value, 0.0)
                return carry + jnp.sum(value * value, axis=0)

            squares = lax.fori_loop(0, blocks, square_part, jnp.zeros((z.tj, z.cp), f32))
            own_var = jnp.sum(squares, axis=0, keepdims=True) * (1.0 / own_cells)
            for tile in range(z.ct):
                lanes = slice(LANES * tile, LANES * (tile + 1))
                r.msg[layer, tile : tile + 1, :] = own_mean[:, lanes]
                r.msg[layer, z.ct + tile : z.ct + tile + 1, :] = own_var[:, lanes]
            exchange_start(layer)
            weights_across(layer, "j")
            weights_across(layer, "m")
            weights_pair(layer, z.join_kind)
            exchange_wait(layer)
            stats = r.stats[layer]
            mean, var = combine(stats[:, 0 : z.ct, :], stats[:, z.ct : 2 * z.ct, :])
            mean = wide_row([mean[t : t + 1] for t in range(z.ct)])
            var = wide_row([var[t : t + 1] for t in range(z.ct)])
        inv_std = lax.rsqrt(var + epsilon)
        r.mv[layer, 0:1, :] = mean
        r.mv[layer, 1:2, :] = var
        r.mv[layer, 2:3, :] = inv_std
        scale = inv_std * param(layer, 9)
        shift = param(layer, 10)

        def norm_part(t, layer=layer, mean=mean, scale=scale, shift=shift):
            lines = pl.ds(t * z.step, z.step)
            active, slope = gelu_both((r.a[layer, lines] - mean) * scale + shift)
            r.sz[layer, lines] = slope
            b, start = place_of(t * z.step)
            value = jnp.where(real_column, active, 0.0)
            r.u[lines] = value

        loop(blocks, norm_part)

        def add_part(b, layer=layer):
            value = r.u[pl.ds(b * z.high, z.high)] + r.x[layer, b, 1 : z.high + 1]
            r.u[pl.ds(b * z.high, z.high)] = value
            r.cat[layer, 0, b] = value.reshape(z.rb, z.cp).astype(bf16)

        loop(z.own, add_part)
        if layer == 0:
            weights_across(0, "j")
            weights_across(0, "m")
            if layers > 1:
                weights_along(1, "j")
                weights_along(1, "m")

        def mix_part(b, layer=layer):
            low = r.cat[layer, 0, b]
            for which in range(2):
                value = dot_nn(r.mix[layer, 2 * which], low) + r.mixb[layer, which, :, 0:1]
                r.cat[layer, 1 + which, b] = value.astype(bf16)

        loop(z.own, mix_part)
        weights_pair(layer, z.join_kind)
        weights_ready(layer, z.join_kind)
        weights_pair(layer, "m")
        if 0 < layer < layers - 1:
            weights_along(layer + 1, "j")
            weights_along(layer + 1, "m")

        def join_part(b, layer=layer):
            value = dot_nn(r.cat[layer, 0, b], r.jf[layer, 0])
            value = value + dot_nn(r.cat[layer, 1, b], r.jf[layer, 1])
            value = value + dot_nn(r.cat[layer, 2, b], r.jf[layer, 2])
            r.w[pl.ds(b * z.high, z.high)] = value.reshape(z.high, z.tj, z.cp)

        loop(z.own, join_part)

        def token_part(t, layer=layer):
            lines = pl.ds(t * z.step, z.step)
            value = r.w[lines] + r.u[lines] + param(layer, 11)
            r.w[lines] = value
            mean = jnp.sum(value, axis=2, keepdims=True) * (1.0 / z.channels)
            away = jnp.where(real_lane, value - mean, 0.0)
            var = jnp.sum(away * away, axis=2, keepdims=True) * (1.0 / z.channels)
            inv = lax.rsqrt(var + epsilon)
            what = away * inv
            r.what[layer, lines] = what
            r.inv[layer, lines] = jnp.broadcast_to(inv, (z.step, z.tj, LANES))
            r.yb[layer, lines] = (what * param(layer, 12) + param(layer, 13)).astype(bf16)

        loop(blocks, token_part)
        weights_ready(layer, "m")

        def mlp_part(b, layer=layer):
            lines = pl.ds(b * z.high, z.high)
            low = r.yb[layer, lines].reshape(z.rb, z.cp)
            total = None
            for block in range(z.nkg):
                parts = slice(block * z.kg, (block + 1) * z.kg)
                rising = r.wt["m"][layer, parts, 0 : z.fl, :].reshape(z.ft, z.cp)
                hidden = dot_nt(low, rising) + r.bi[layer, block, 0:1, :]
                active, slope = gelu_both(hidden)
                r.hs[layer, block, b] = slope
                active = active.astype(bf16)
                r.gb[layer, block, b] = active
                falling = r.wt["m"][layer, parts, z.fl : 2 * z.fl, :].reshape(z.ft, z.cp)
                term = dot_nn(active, falling)
                total = term if total is None else total + term
            value = total.reshape(z.high, z.tj, z.cp) + r.w[lines] + param(layer, 14)
            value = jnp.where(real_part, value, 0.0)
            if layer + 1 < layers:
                r.x[layer + 1, b, 1 : z.high + 1] = value
            else:
                r.o[lines] = value

        real_part = lax.broadcasted_iota(jnp.int32, (z.high, z.tj, z.cp), 1) < z.wide
        loop(z.own, mlp_part)

        if layer == 0:
            def take_cotangent(n):
                def line(h):
                    r.xl[n, h + 1, 0 : z.wide, 0 : z.cl] = r.cotangent[n, h]

                loop(z.high, line)
                r.stage[1, lax.div(n, z.own), lax.rem(n, z.own)] = r.xl[n, 1 : z.high + 1].astype(bf16)

            loop(z.group, take_cotangent)
            swap_start(1)
            own_tile(1)

    def take_o(b, start, tile):
        return r.o[pl.ds(b * z.high + start, z.lines), :, LANES * tile : LANES * (tile + 1)]

    pack(2, take_o)
    swap_start(2)
    own_tile(2)
    swap_wait(1)
    unpack(1, store_gx)

    for layer in reversed(range(layers)):
        above = layer + 1 if layer + 1 < layers else None

        def start_part(t, carry):
            lines = pl.ds(t * z.step, z.step)
            value = r.gx[lines]
            r.gob[lines] = value.astype(bf16)
            return carry + jnp.sum(value, axis=0)

        total = lax.fori_loop(0, blocks, start_part, jnp.zeros((z.tj, z.cp), f32))
        r.sg[12:13, :] = jnp.sum(total, axis=0, keepdims=True)
        low_out = r.gob[...].reshape(z.rows, z.cp)

        for block in range(z.nkg):
            parts = slice(block * z.kg, (block + 1) * z.kg)
            falling = r.wt["m"][layer, parts, z.fl : 2 * z.fl, :].reshape(z.ft, z.cp)
            rising = r.wt["m"][layer, parts, 0 : z.fl, :].reshape(z.ft, z.cp)

            def back_part(b, carry, layer=layer, block=block, falling=falling, rising=rising):
                lines = pl.ds(b * z.high, z.high)
                low = r.gob[lines].reshape(z.rb, z.cp)
                value = dot_nt(low, falling) * r.hs[layer, block, b]
                low = value.astype(bf16)
                r.gh[b] = low
                term = dot_nn(low, rising).reshape(z.high, z.tj, z.cp)
                r.o[lines] = term if block == 0 else r.o[lines] + term
                return carry + jnp.sum(value, axis=0, keepdims=True)

            total = lax.fori_loop(0, z.own, back_part, jnp.zeros((1, z.ft), f32))
            r.bg[0:1, block * z.ft : (block + 1) * z.ft] = total
            low_hidden = r.gh[...].reshape(z.rows, z.ft)
            low_in = r.yb[layer].reshape(z.rows, z.cp)
            value = dot_tn(low_hidden, low_in).astype(bf16).reshape(z.kg, z.fl, z.cp)
            r.gr["m"][layer, parts, 0 : z.fl, :] = value
            low_active = r.gb[layer, block].reshape(z.rows, z.ft)
            value = dot_tn(low_active, low_out).astype(bf16).reshape(z.kg, z.fl, z.cp)
            r.gr["m"][layer, parts, z.fl : 2 * z.fl, :] = value
        if z.join_kind != "m":
            reduce_pair(layer, "m")
        if above is not None:
            reduce_along(above, "m")
            reduce_along(above, "j")

        def token_back(t, carry, layer=layer):
            lines = pl.ds(t * z.step, z.step)
            gain_sum, bias_sum, join_sum = carry
            gy, what = r.o[lines], r.what[layer, lines]
            inv = r.inv[layer, lines][:, :, 0:1]
            scaled = gy * param(layer, 12)
            plain = jnp.sum(scaled, axis=2, keepdims=True) * (1.0 / z.channels)
            cross = jnp.sum(scaled * what, axis=2, keepdims=True) * (1.0 / z.channels)
            value = r.gx[lines] + inv * (jnp.where(real_lane, scaled - plain, 0.0) - what * cross)
            r.gw[lines] = value
            r.gsb[lines] = value.astype(bf16)
            return (
                gain_sum + jnp.sum(gy * what, axis=0),
                bias_sum + jnp.sum(gy, axis=0),
                join_sum + jnp.sum(value, axis=0),
            )

        zero = jnp.zeros((z.tj, z.cp), f32)
        gain_sum, bias_sum, join_sum = lax.fori_loop(0, blocks, token_back, (zero, zero, zero))
        r.sg[9:10, :] = jnp.sum(join_sum, axis=0, keepdims=True)
        r.sg[10:11, :] = jnp.sum(gain_sum, axis=0, keepdims=True)
        r.sg[11:12, :] = jnp.sum(bias_sum, axis=0, keepdims=True)

        low_join = r.gsb[...].reshape(z.rows, z.cp)
        for branch in range(3):
            value = dot_tn(r.cat[layer, branch].reshape(z.rows, z.cp), low_join)
            for part in range(nk):
                row = z.join_row + branch * z.clp
                r.gr[z.join_kind][layer, part, row : row + z.cl, :] = value[
                    part * z.cl : (part + 1) * z.cl
                ].astype(bf16)
        reduce_pair(layer, z.join_kind)

        def mix_back(b, carry, layer=layer):
            lines = pl.ds(b * z.high, z.high)
            low = r.gsb[lines].reshape(z.rb, z.cp)
            total = r.gw[lines].reshape(z.rb, z.cp) + dot_nt(low, r.jf[layer, 0])
            tables, sums = [], []
            for which in range(2):
                value = dot_nt(low, r.jf[layer, 1 + which])
                back = value.astype(bf16)
                total = total + dot_nn(r.mix[layer, 2 * which + 1], back)
                tables.append(carry[which] + dot_nt(back, r.cat[layer, 0, b]))
                sums.append(carry[2 + which] + jnp.sum(value, axis=1, keepdims=True))
            r.gu[lines] = total.reshape(z.high, z.tj, z.cp)
            return (*tables, *sums)

        square, column = jnp.zeros((z.rb, z.rb), f32), jnp.zeros((z.rb, 1), f32)
        rows_table, cols_table, rows_sum, cols_sum = lax.fori_loop(
            0, z.own, mix_back, (square, square, column, column)
        )

        inv_std = r.mv[layer, 2:3, :]
        mean = r.mv[layer, 0:1, :]

        def gate_back(t, carry, layer=layer, mean=mean, inv_std=inv_std):
            lines = pl.ds(t * z.step, z.step)
            value = r.gu[lines] * r.sz[layer, lines]
            r.gz[lines] = value
            centred = (r.a[layer, lines] - mean) * inv_std
            return carry[0] + jnp.sum(value, axis=0), carry[1] + jnp.sum(value * centred, axis=0)

        first, second = lax.fori_loop(0, blocks, gate_back, (zero, zero))
        first = jnp.sum(first, axis=0, keepdims=True)
        second = jnp.sum(second, axis=0, keepdims=True)
        slot = layers + layer
        for tile in range(z.ct):
            lanes = slice(LANES * tile, LANES * (tile + 1))
            r.msg[slot, tile : tile + 1, :] = first[:, lanes]
            r.msg[slot, z.ct + tile : z.ct + tile + 1, :] = second[:, lanes]
        exchange_start(slot)

        rows_table = jnp.where(same_wide, rows_table, 0.0).reshape(z.high, z.tj, z.rb)
        rows_table = jnp.sum(rows_table, axis=1)
        rows_table = lax.dot_general(
            rows_table, pick_high, (((1,), (0,)), ((), ())), preferred_element_type=f32, precision=lax.Precision.HIGHEST
        )
        cols_table = jnp.sum(jnp.where(same_high, cols_table, 0.0).reshape(z.high, z.tj, z.rb), axis=0)
        cols_table = lax.dot_general(
            cols_table, pick_wide, (((1,), (0,)), ((), ())), preferred_element_type=f32, precision=lax.Precision.HIGHEST
        )
        r.mg[0 : z.high, 0:16] = rows_table
        r.mg[:, 16:32] = cols_table
        r.mg[0 : z.high, 32:33] = jnp.sum(rows_sum.reshape(z.high, z.tj, 1), axis=1)
        r.mg[:, 33:34] = jnp.sum(cols_sum.reshape(z.high, z.tj, 1), axis=0)
        reduce_across(layer, "m")
        reduce_across(layer, "j")
        if above is not None:
            spread_across(above, "m")
            spread_across(above, "j")

        exchange_wait(slot)
        stats = jnp.sum(r.stats[slot], axis=0)
        bias_total = wide_row([stats[t : t + 1] for t in range(z.ct)])
        gain_total = wide_row([stats[z.ct + t : z.ct + t + 1] for t in range(z.ct)])
        r.mv[layer, 3:4, :] = gain_total
        r.mv[layer, 4:5, :] = bias_total
        factor = inv_std * param(layer, 9)
        plain = bias_total * (1.0 / z.cells)
        cross = gain_total * (1.0 / z.cells) * inv_std

        def conv_gate(b, layer=layer, mean=mean, factor=factor, plain=plain, cross=cross):
            lines = pl.ds(b * z.high, z.high)
            value = r.gz[lines] - plain - (r.a[layer, lines] - mean) * cross
            r.ga[b, 1 : z.high + 1] = jnp.where(real_part, value * factor, 0.0)

        loop(z.own, conv_gate)

        def conv_back(t, layer=layer):
            b, part = lax.div(t, z.high // z.lines), lax.rem(t, z.high // z.lines)
            start = part * z.lines
            lines = pl.ds(b * z.high + start, z.lines)
            for tile in range(z.ct):
                lanes = slice(LANES * tile, LANES * (tile + 1))
                taps = [r.pf[layer, 8 - row : 9 - row, lanes] for row in range(9)]
                value = conv(r.ga[b, pl.ds(start, z.lines + 2), :, lanes], taps)
                r.gx[lines, :, lanes] = jnp.where(inside, value + r.gu[lines, :, lanes], 0.0)

        loop(z.own * (z.high // z.lines), conv_back)

        if layer == 0:

            def take_gx(b, start, tile):
                return r.gx[pl.ds(b * z.high + start, z.lines), :, LANES * tile : LANES * (tile + 1)]

            pack(3, take_gx)
            swap_start(3)
            own_tile(3)

        for tile in range(z.ct):
            lanes = slice(LANES * tile, LANES * (tile + 1))

            def kernel_part(t, carry, layer=layer, lanes=lanes):
                b, part = lax.div(t, z.high // z.lines), lax.rem(t, z.high // z.lines)
                start = part * z.lines
                lines = r.x[layer, b, pl.ds(start, z.lines + 2), :, lanes]
                upstream = r.ga[b, pl.ds(start + 1, z.lines), :, lanes]
                shifted = (pltpu.roll(lines, 1, 1), lines, pltpu.roll(lines, z.tj - 1, 1))
                return tuple(
                    carry[3 * down + side]
                    + jnp.sum(jnp.sum(shifted[side][down : down + z.lines] * upstream, axis=0), axis=0, keepdims=True)
                    for down in range(3)
                    for side in range(3)
                )

            totals = lax.fori_loop(
                0,
                z.own * (z.high // z.lines),
                kernel_part,
                tuple(jnp.zeros((1, LANES), f32) for _ in range(9)),
            )
            for row in range(9):
                r.sg[row : row + 1, lanes] = totals[row]

        tiles = [r.sg[:, LANES * tile : LANES * (tile + 1)] for tile in range(z.ct)]
        for part in range(nk):
            r.sgm[layer, part, 0:16, :] = cut(tiles, part * z.cl, z.cl)
            for tile in range(z.ftiles):
                start = part * z.fl + LANES * tile
                width = min(LANES, z.fl - LANES * tile)
                hidden = [
                    r.bg[:, LANES * t : min(LANES * (t + 1), nk * z.fl)] for t in range(-(-nk * z.fl // LANES))
                ]
                r.sgm[layer, part, 13 + tile : 14 + tile, :] = cut(hidden, start, width)[0:1]
            r.sgm[layer, part, 16:32, :] = r.mg[...]
        r.sgk[layer, k] = r.sgm[layer, k]
        for step in range(1, nk):
            other = lax.rem(k + step, nk)
            send(("s1", layer), r.sgm.at[layer, other], r.sgk.at[layer, k], at(i, other))

    def small_across(layer):
        arrived(("s1", layer), r.sgk.at[layer, pl.ds(0, nk - 1)])
        r.sgz[layer] = jnp.sum(r.sgk[layer], axis=0)
        r.sgi[layer, i] = r.sgz[layer]

        def one(j):
            send(("s2", layer), r.sgz.at[layer], r.sgi.at[layer, i], at(lax.rem(i + j, ni), k))

        loop(ni, one, 1)

    def small_ready(layer):
        arrived(("s2", layer), r.sgi.at[layer, pl.ds(0, ni - 1)])
        r.out_s[layer, 0:32, :] = jnp.sum(r.sgi[layer], axis=0)
        tiles = [r.mv[layer, :, LANES * tile : LANES * (tile + 1)] for tile in range(z.ct)]
        mine = jnp.zeros((8, LANES), f32)
        for part in range(nk):
            mine = mine + jnp.where(k == part, cut(tiles, part * z.cl, z.cl), 0.0)
        r.out_s[layer, 32:40, :] = mine

    for layer in reversed(range(layers)):
        small_across(layer)
    reduce_along(0, "m")
    reduce_along(0, "j")
    for layer in range(1, layers):
        spread_pair(layer, "m")
        spread_pair(layer, "j")
    spread_across(0, "m")
    spread_across(0, "j")
    swap_wait(2)
    r.out_y[...] = r.land[2]
    for layer in range(1, layers):
        small_ready(layer)
        spread_ready(layer, "m")
        spread_ready(layer, "j")
    small_ready(0)
    swap_wait(3)
    r.out_g[...] = r.land[3]
    spread_pair(0, "m")
    spread_pair(0, "j")
    spread_ready(0, "m")
    spread_ready(0, "j")

    for number, ref in sends:
        pltpu.make_async_remote_copy(
            src_ref=ref,
            dst_ref=ref,
            send_sem=ssem.at[number],
            recv_sem=rsem.at[number],
            device_id=at(partner, k),
            device_id_type=MESH,
        ).wait_send()


EVENTS = 80


def on_device(ni, nk, *args):
    images, conv_kernel, weight_in = args[0], args[1], args[12]
    running_mean, running_var, cotangent = args[16:19]
    z = Sizes(ni, nk, images, conv_kernel, weight_in)
    inputs = (*args[:16], cotangent)
    out_shape = (
        jax.ShapeDtypeStruct((nk, z.own, z.high, z.tj, LANES), bf16),
        jax.ShapeDtypeStruct((nk, z.own, z.high, z.tj, LANES), bf16),
        jax.ShapeDtypeStruct((z.layers, SMALL_ROWS, LANES), f32),
        *(jax.ShapeDtypeStruct((z.layers, ni * part, z.cp), bf16) for part in z.parts.values()),
    )
    vmem = pl.BlockSpec(memory_space=pltpu.VMEM)
    shapes, groups = scratch_list(z)
    scratch = [pltpu.VMEM(shape, kind) for table in (shapes, *groups) for shape, kind in table.values()]
    scratch += [pltpu.SemaphoreType.DMA((EVENTS,)), pltpu.SemaphoreType.DMA((EVENTS,))]
    out_y, out_g, out_s, *grads = pl.pallas_call(
        functools.partial(whole, z),
        out_shape=out_shape,
        in_specs=[vmem] * len(inputs),
        out_specs=(vmem,) * len(out_shape),
        scratch_shapes=scratch,
        compiler_params=pltpu.CompilerParams(
            collective_id=0, has_side_effects=True, vmem_limit_bytes=62 * 2**20
        ),
    )(*inputs)
    grads = dict(zip(z.parts, grads, strict=True))
    out_m, out_j = grads["m"], grads[z.join_kind][:, z.join_row :]
    shape = (z.group, z.high, z.tj, LANES)
    output = out_y.reshape(shape)[:, :, : z.wide, : z.cl]
    images_grad = out_g.reshape(shape)[:, :, : z.wide, : z.cl].astype(f32)
    rising = out_m[:, : z.fl, : z.channels].astype(f32).transpose(0, 2, 1)
    falling = out_m[:, z.fl : 2 * z.fl, : z.channels].astype(f32)
    join = out_j[:, : 3 * z.clp].reshape(z.layers, 3, z.clp, z.cp)[:, :, : z.cl, : z.channels].astype(f32)
    kernel_grad = out_s[:, :9, : z.cl].reshape(z.layers, 3, 3, z.cl)
    hidden_bias = out_s[:, 13 : 13 + z.ftiles, :].reshape(z.layers, -1)[:, : z.fl]
    mean, var = out_s[:, 32, : z.cl], out_s[:, 33, : z.cl]
    return (
        output,
        images_grad,
        kernel_grad,
        out_s[:, 35, : z.cl],
        out_s[:, 36, : z.cl],
        out_s[:, 16 : 16 + z.high, : z.high],
        out_s[:, 16 : 16 + z.high, 32],
        out_s[:, 16 : 16 + z.wide, 16 : 16 + z.wide],
        out_s[:, 16 : 16 + z.wide, 33],
        join,
        out_s[:, 9, : z.cl],
        out_s[:, 10, : z.cl],
        out_s[:, 11, : z.cl],
        rising,
        hidden_bias,
        falling,
        out_s[:, 12, : z.cl],
        0.9 * running_mean + 0.1 * mean,
        0.9 * running_var + 0.1 * var * (z.cells / (z.cells - 1.0)),
    )


def solution(mesh):
    return jax.shard_map(
        functools.partial(on_device, mesh.shape["img"], mesh.shape["ch"]),
        mesh=mesh,
        in_specs=(
            P("img", None, None, "ch"),
            P(None, None, None, "ch"),
            P(None, "ch"),
            P(None, "ch"),
            P(),
            P(),
            P(),
            P(),
            P(None, None, "ch", None),
            P(None, "ch"),
            P(None, "ch"),
            P(None, "ch"),
            P(None, None, "ch"),
            P(None, "ch"),
            P(None, "ch", None),
            P(None, "ch"),
            P(None, "ch"),
            P(None, "ch"),
            P("img", None, None, "ch"),
        ),
        out_specs=(
            P("img", None, None, "ch"),
            P("img", None, None, "ch"),
            P(None, None, None, "ch"),
            P(None, "ch"),
            P(None, "ch"),
            P(),
            P(),
            P(),
            P(),
            P(None, None, "ch", None),
            P(None, "ch"),
            P(None, "ch"),
            P(None, "ch"),
            P(None, None, "ch"),
            P(None, "ch"),
            P(None, "ch", None),
            P(None, "ch"),
            P(None, "ch"),
            P(None, "ch"),
        ),
        check_vma=False,
    )
```

time: 653 us -> 158 us (0.24); the launches traced: 643 us -> 158 us
  blocking collectives: 307 us -> 0 us
  Pallas kernels: 0 us -> 139 us
  waiting for transfers between devices: 116 us -> 0 us
  other arithmetic: 72.5 us -> 6.26 us
  matrix products: 60.6 us -> 0 us
  local copies, waits for them, and re-layouts: 71.1 us -> 11.7 us
  between operations: 16.3 us -> 0.73 us
    psum x10 -> x0, blocking collectives: 172 us -> none  [the longest x4 67.8 us: row_totals(): return lax.psum((first_sum, second_sum), 'ch')]
    pallas_call x0 -> x1, Pallas kernels: none -> 139 us  [on_device(): pl.pallas_call(functools.partial(whole, z), out_shape=out_shape, in_specs...]
    all_gather x6 -> x0, blocking collectives: 134 us -> none  [channel_gather(): return lax.all_gather(values, 'ch', axis=1, tiled=True)]
    reduce_scatter x6 -> x0, waiting for transfers between devices: 75.8 us -> none  [channel_sum(): lax.psum_scatter(values.astype(jnp.bfloat16), 'ch', scatter_dimension=1,...]
    dot_general x30 -> x0, matrix products: 60.6 us -> none  [the longest x2 9.88 us: axial_back(): jnp.einsum('ij,biwc->bjwc', rows_weight, grad_rows, precision=highest)]
    psum x1 -> x0, waiting for transfers between devices: 39.9 us -> none  [on_device(): lax.psum(ffn_parts[0].astype(jnp.bfloat16), 'img').astype(jnp.float32)]
    reduce_sum x20 -> x0, other arithmetic: 35.6 us -> none  [the longest x2 9.54 us: depthwise_back(): jnp.sum(padded_src[:, offset_row:offset_row + extent, offset_col:offset_c...]
    another operation x20 -> x0, local copies, waits for them, and re-layouts: 14.9 us -> none  [the longest x12 11.9 us: on_device(): jnp.stack([after_conv, along_rows, along_cols])]
  transfers between devices with their start and end apart: 7 -> 0, of which waited for: 5 -> 0; matrix products, arithmetic and copies ran while one was open for 10% -> 0% of each run, Pallas kernels for 0% -> 0%
where the time goes in v1:
time: 158 us
  Pallas kernels  139 us (88%)
  local copies, waits for them, and re-layouts  11.7 us (7%)
  other arithmetic  6.26 us (4%)
    pallas_call x1, Pallas kernels, on_device(): pl.pallas_call(functools.partial(whole, z), out_shape=out_shape, in_specs...  139 us
    unnamed x31, local copies, waits for them, and re-layouts  9.42 us

profile of v1, /device:TPU:0, one launch (start us, length us, event | category | flops | bytes accessed | tf_op | source)
XLA Modules:
  0.0 157.8 jit_solution(4019654246180884708)
XLA Ops:
  0.7 0.0 copy-start.3
  0.7 2.3 %copy.54.refs_16_ = f32[8,14,14,80]{3,2,1,0:T(8,128)} copy(f32[8,14,14,80]{3,0,2,1:T(8,128)} %param.37) | data formatting | bytes 1003520 | tf_op args[18]
  3.0 0.0 copy-done.3
  3.0 0.0 copy-start.5
  3.0 0.8 copy.50.refs_0_
  3.8 0.0 copy-done.5
  3.8 0.0 copy-start.6
  3.8 0.6 copy.52.refs_4_
  4.4 0.1 copy-done.6
  4.5 0.0 copy-start.7
  4.5 0.6 copy.53.refs_6_
  5.1 0.1 copy-done.7
  5.2 0.6 copy.51.refs_1_
  5.8 139.1 %shard_map.330 = (bf16[4,2,14,16,128]{4,3,2,1,0:T(8,128)(2,1)}, bf16[4,2,14,16,128]{4,3,2,1,0:T(8,128)(2,1)}, f32[2,40,128]{2,1,0:T(8,128)}, bf16[2,640,384]{2,1,0:T(8,128)(2,1)}, bf16[2,256,384]{2,1,0:T(8,128)(2,1)}) custom-call(bf16[8,14,14,80]{3,2,1,0:T(8,128)(2,1)} %copy.50.refs_0_, bf16[2,3,3,80]{3,2,1,0:T(4,128)(2,1)} %copy.51.refs_1_, ...), custom_call_target="tpu_custom_call" | custom-call | tf_op jit(solution)/shard_map/pallas_call | solution.py:1096
  144.9 1.5 slice_multiply_fusion.1
  146.4 0.0 copy-start.8
  146.4 0.0 copy-start.9
  146.4 0.0 copy-start.2
  146.4 0.9 copy.58
  147.3 0.0 copy-done.8
  147.3 0.0 copy-done.9
  147.3 0.6 fusion.1
  147.9 0.0 copy-done.2
  147.9 0.1 fusion.2
  148.0 0.6 copy.59
  148.6 0.6 copy.60
  149.2 0.7 slice_reduce_fusion
  149.9 0.6 copy.57
  150.5 0.6 copy.67
  151.1 2.3 %slice_convert_fusion = (f32[2,320,320]{2,1,0:T(8,128)}, f32[2,320,320]{1,2,0:T(8,128)S(1)}) fusion(bf16[2,640,384]{2,1,0:T(8,128)(2,1)} %get-tuple-element.28), kind=kLoop, calls=%fused_computation.1 | loop fusion | flops 409600 | bytes 2457600 | tf_op jit(solution)/shard_map/convert_element_type | solution.py:1112
  153.3 0.0 copy-start.4
  153.3 1.3 copy.61
  154.6 0.0 copy-done.4
  154.7 0.0 copy-start.1
  154.7 0.9 slice_convert_fusion.1
  155.6 0.3 copy-done.1
  155.9 0.0 copy-start
  155.9 1.0 copy_convert_fusion
  156.9 0.0 copy-done
  156.9 0.9 copy.62
  (3 shorter events, 0.0 us)
Async XLA Ops:
  0.7 2.3 %copy-start.3 = (bf16[8,14,14,80]{3,0,2,1:T(8,128)(2,1)S(1)}, bf16[8,14,14,80]{3,0,2,1:T(8,128)(2,1)}, u32[]{:S(2)}) copy-start(bf16[8,14,14,80]{3,0,2,1:T(8,128)(2,1)} %param.19) | copy-start | bytes 752644
  3.0 0.8 copy-start.5
  3.8 0.7 copy-start.6
  4.5 0.7 copy-start.7
  146.4 0.9 copy-start.8
  146.4 0.9 copy-start.9
  146.4 1.5 copy-start.2
  153.3 1.3 copy-start.4
  154.7 1.2 copy-start.1
  155.9 1.0 copy-start

commit v2 on v1

--- a/solution.py
+++ b/solution.py
@@ -80,12 +80,44 @@
     return value if width == LANES else jnp.where(lane < width, value, 0.0)
 
 
+def line_groups(z, body):
+    def run(g, carry):
+        body(g * z.gl, g * z.gt, z.gl, z.gt)
+        return carry
+
+    if z.full:
+        lax.fori_loop(0, z.full, run, 0)
+    if z.rest:
+        body(z.full * z.gl, z.full * z.gt, z.rest, z.rest_t)
+
+
+def pack(z, stage, target, line):
+    def group(first, tile, lines, tiles):
+        values = assemble([(line(first + j), j * z.cl, z.cl) for j in range(lines)], tiles)
+        for t in range(tiles):
+            stage[target, tile + t] = values[t].astype(bf16)
+
+    line_groups(z, group)
+
+
+def unpack(z, land, store):
+    def group(first, tile, lines, tiles):
+        sources = [[land[k, tile + t].astype(f32) for t in range(tiles)] for k in range(z.nk)]
+        for j in range(lines):
+            store(
+                first + j,
+                assemble([(cut(source, j * z.cl, z.cl), k * z.cl, z.cl) for k, source in enumerate(sources)], z.ct),
+            )
+
+    line_groups(z, group)
+
+
 class Sizes:
     def __init__(self, ni, nk, images, conv_kernel, weight_in):
         self.ni, self.nk, self.nd = ni, nk, ni * nk
         self.chips = ni // 2
-        self.group, self.high, self.wide, self.cl = images.shape
-        self.layers = conv_kernel.shape[0]
+        self.high, self.wide, self.group, self.cl = images.shape
+        self.layers = conv_kernel.shape[2]
         self.own = self.group // nk
         self.channels = weight_in.shape[1]
         self.fl = weight_in.shape[2]
@@ -115,6 +147,11 @@
         self.step = next(n for n in (4, 2, 1) if self.bh % n == 0)
         self.lines = next(n for n in (7, 4, 2, 1) if self.high % n == 0)
         self.stat = up(2 * self.ct, 8)
+        self.gl = next(n for n in range(1, LANES + 1) if n * self.cl % LANES == 0)
+        self.gt = self.gl * self.cl // LANES
+        self.full, self.rest = divmod(self.bh, self.gl)
+        self.rest_t = -(-self.rest * self.cl // LANES)
+        self.packed = self.full * self.gt + self.rest_t
 
 
 PARAM_ROWS = 16
@@ -122,9 +159,10 @@
 
 
 def scratch_list(z):
-    tile = (z.own, z.high, z.tj, LANES)
+    tile = (z.packed, z.tj, LANES)
     layer, rows, cp = z.layers, z.rows, z.cp
     shapes = dict(
+        tmp=((z.high, z.wide * z.group, LANES), f32),
         xl=((z.group, z.high + 2, z.tj, LANES), f32),
         al=((z.group, z.high, z.tj, LANES), f32),
         stage=((4, z.nk) + tile, bf16),
@@ -428,7 +466,7 @@
         arrived(("r5", layer, kind), r.fin[kind].at[layer, pl.ds(0, z.chips * rps(kind))])
         r.outs[kind][layer] = r.fin[kind][layer]
 
-    cleared = [r.xl, r.x, r.ga, r.par, r.pf, r.bi, r.mixs, r.mg, r.sg, r.bg, r.sgm]
+    cleared = [r.tmp, r.xl, r.x, r.ga, r.par, r.pf, r.bi, r.mixs, r.mg, r.sg, r.bg, r.sgm]
     for ref in cleared + list(r.gr.values()):
         if len(ref.shape) > 3:
 
@@ -442,14 +480,20 @@
     tile_row = lax.broadcasted_iota(jnp.int32, (z.tj, LANES), 0)
     inside = tile_row < z.wide
 
-    def take_image(n):
+    def take(ref, slot):
         def line(h):
-            r.xl[n, h + 1, 0 : z.wide, 0 : z.cl] = r.images[n, h].astype(f32)
+            r.tmp[h, :, 0 : z.cl] = ref[h].astype(f32).reshape(z.wide * z.group, z.cl)
+            for n in range(z.group):
+                r.xl[n, h + 1, 0 : z.wide, :] = r.tmp[h, pl.ds(n, z.wide, stride=z.group), :]
 
         loop(z.high, line)
-        r.stage[0, lax.div(n, z.own), lax.rem(n, z.own)] = r.xl[n, 1 : z.high + 1].astype(bf16)
-
-    loop(z.group, take_image)
+
+        def target(d):
+            pack(z, r.stage.at[slot], d, lambda m: r.xl[d * z.own + lax.div(m, z.high), lax.rem(m, z.high) + 1])
+
+        loop(nk, target)
+
+    take(r.images, 0)
 
     small = [
         (9, r.bn_gain),
@@ -466,7 +510,9 @@
     values = r.bias_in[...].astype(f32)
     for layer in range(layers):
         for tap in range(3):
-            r.par[layer, 3 * tap : 3 * tap + 3, 0 : z.cl] = r.conv_kernel[layer, tap].astype(f32)
+            for side in range(3):
+                row = 3 * tap + side
+                r.par[layer, row : row + 1, 0 : z.cl] = r.conv_kernel[tap, side].astype(f32)[layer : layer + 1]
         for tile in range(z.ftiles):
             stop = min(z.fl, LANES * (tile + 1))
             r.par[layer, PARAM_ROWS + tile : PARAM_ROWS + tile + 1, 0 : stop - LANES * tile] = values[
@@ -501,15 +547,6 @@
     total = lax.fori_loop(0, z.group, square_local, jnp.zeros((z.tj, LANES), f32))
     local_var = jnp.sum(total, axis=0, keepdims=True) * (1.0 / local_cells)
     r.msg[0] = jnp.concatenate([local_mean, local_var, jnp.zeros((z.stat - 2, LANES), f32)], axis=0)
-
-    pl.semaphore_wait(barrier, nd - 1)
-
-    swap_start(0)
-    exchange_start(0)
-    r.pars[k] = r.par[...]
-    for step in range(1, nk):
-        send("par", r.par, r.pars.at[k], at(i, lax.rem(k + step, nk)))
-    own_tile(0)
 
     blank = jnp.zeros((z.cl, z.cp - z.channels), f32)
     blank_hidden = jnp.zeros((z.fl, z.cp - z.channels), f32)
@@ -529,9 +566,17 @@
             if z.cp > z.channels:
                 value = jnp.concatenate([value, blank_hidden], axis=1)
             r.wt["m"][layer, k, place : place + z.fl, :] = value.astype(bf16)
-        if layer == 0:
-            for kind in ("j", "m"):
-                weights_along(0, kind)
+
+    pl.semaphore_wait(barrier, nd - 1)
+
+    exchange_start(0)
+    r.pars[k] = r.par[...]
+    for step in range(1, nk):
+        send("par", r.par, r.pars.at[k], at(i, lax.rem(k + step, nk)))
+    weights_along(0, "j")
+    weights_along(0, "m")
+    swap_start(0)
+    own_tile(0)
 
     select_row = lax.broadcasted_iota(jnp.int32, (z.rb, 16), 0)
     select_col = lax.broadcasted_iota(jnp.int32, (z.rb, 16), 1)
@@ -549,13 +594,16 @@
                 (r.mix_cols, r.mix_cols_bias, low_wide, same_high, z.wide),
             )
         ):
-            r.mixs[which, 0:extent, 0:extent] = maps[layer].astype(f32)
+            r.mixs[which, 0:extent, 0:extent] = maps[:, layer, :].astype(f32)
             table = r.mixs[which].astype(bf16)
             for turned, half in ((0, dot_nn(pick, table)), (1, dot_nt(pick, table))):
                 spread = dot_nt(half.astype(bf16), pick)
                 r.mix[layer, 2 * which + turned] = jnp.where(same, spread, 0.0).astype(bf16)
             r.mixs[2 + which, 0:1, 0:extent] = shifts[layer : layer + 1, :].astype(f32)
             r.mixb[layer, which] = dot_nt(pick, r.mixs[2 + which, 0:8, :].astype(bf16))
+
+    weights_across(0, "j")
+    weights_across(0, "m")
 
     exchange_wait(0)
     arrived("par", r.pars.at[pl.ds(0, nk - 1)])
@@ -600,45 +648,27 @@
     def place_of(t):
         return lax.div(t, z.high), lax.rem(t, z.high)
 
-    def unpack(slot, store):
-        def image(b):
-            def lines(part):
-                start = part * z.lines
-                tiles = assemble(
-                    [
-                        (r.land[slot, source, b, pl.ds(start, z.lines)].astype(f32), source * z.cl, z.cl)
-                        for source in range(nk)
-                    ],
-                    z.ct,
-                )
-                store(b, start, tiles)
-
-            loop(z.high // z.lines, lines)
-
-        loop(z.own, image)
-
-    def store_x(b, start, tiles):
+    def store_x(m, tiles):
         for tile in range(z.ct):
-            r.x[0, b, pl.ds(start + 1, z.lines), :, LANES * tile : LANES * (tile + 1)] = tiles[tile]
-
-    def store_gx(b, start, tiles):
+            r.x[0, lax.div(m, z.high), lax.rem(m, z.high) + 1, :, LANES * tile : LANES * (tile + 1)] = tiles[tile]
+
+    def store_gx(m, tiles):
         for tile in range(z.ct):
-            r.gx[pl.ds(b * z.high + start, z.lines), :, LANES * tile : LANES * (tile + 1)] = tiles[tile]
-
-    def pack(slot, take):
-        def image(b):
-            def lines(part):
-                start = part * z.lines
-                tiles = [take(b, start, tile) for tile in range(z.ct)]
-                for target in range(nk):
-                    r.stage[slot, target, b, pl.ds(start, z.lines)] = cut(tiles, target * z.cl, z.cl).astype(bf16)
-
-            loop(z.high // z.lines, lines)
-
-        loop(z.own, image)
-
+            r.gx[m, :, LANES * tile : LANES * (tile + 1)] = tiles[tile]
+
+    def slices_of(ref, slot):
+        for d in range(nk):
+
+            def line(m, d=d):
+                return cut([ref[m, :, LANES * t : LANES * (t + 1)] for t in range(z.ct)], d * z.cl, z.cl)
+
+            pack(z, r.stage.at[slot], d, line)
+
+    if layers > 1:
+        weights_along(1, "j")
+        weights_along(1, "m")
     swap_wait(0)
-    unpack(0, store_x)
+    unpack(z, r.land.at[0], store_x)
 
     own_cells = z.own * z.high * z.wide
 
@@ -689,7 +719,10 @@
             exchange_start(layer)
             weights_across(layer, "j")
             weights_across(layer, "m")
-            weights_pair(layer, z.join_kind)
+            if layer == 1:
+                take(r.cotangent, 1)
+                swap_start(1)
+                own_tile(1)
             exchange_wait(layer)
             stats = r.stats[layer]
             mean, var = combine(stats[:, 0 : z.ct, :], stats[:, z.ct : 2 * z.ct, :])
@@ -718,12 +751,7 @@
             r.cat[layer, 0, b] = value.reshape(z.rb, z.cp).astype(bf16)
 
         loop(z.own, add_part)
-        if layer == 0:
-            weights_across(0, "j")
-            weights_across(0, "m")
-            if layers > 1:
-                weights_along(1, "j")
-                weights_along(1, "m")
+        weights_pair(layer, z.join_kind)
 
         def mix_part(b, layer=layer):
             low = r.cat[layer, 0, b]
@@ -732,7 +760,6 @@
                 r.cat[layer, 1 + which, b] = value.astype(bf16)
 
         loop(z.own, mix_part)
-        weights_pair(layer, z.join_kind)
         weights_ready(layer, z.join_kind)
         weights_pair(layer, "m")
         if 0 < layer < layers - 1:
@@ -762,6 +789,8 @@
 
         loop(blocks, token_part)
         weights_ready(layer, "m")
+        if layer + 1 < layers:
+            weights_across(layer + 1, "j")
 
         def mlp_part(b, layer=layer):
             lines = pl.ds(b * z.high, z.high)
@@ -788,26 +817,33 @@
         real_part = lax.broadcasted_iota(jnp.int32, (z.high, z.tj, z.cp), 1) < z.wide
         loop(z.own, mlp_part)
 
-        if layer == 0:
-            def take_cotangent(n):
-                def line(h):
-                    r.xl[n, h + 1, 0 : z.wide, 0 : z.cl] = r.cotangent[n, h]
-
-                loop(z.high, line)
-                r.stage[1, lax.div(n, z.own), lax.rem(n, z.own)] = r.xl[n, 1 : z.high + 1].astype(bf16)
-
-            loop(z.group, take_cotangent)
-            swap_start(1)
-            own_tile(1)
-
-    def take_o(b, start, tile):
-        return r.o[pl.ds(b * z.high + start, z.lines), :, LANES * tile : LANES * (tile + 1)]
-
-    pack(2, take_o)
-    swap_start(2)
+    if layers == 1:
+        take(r.cotangent, 1)
+        swap_start(1)
+        own_tile(1)
+    slices_of(r.o, 2)
     own_tile(2)
     swap_wait(1)
-    unpack(1, store_gx)
+    unpack(z, r.land.at[1], store_gx)
+
+    def small_across(layer):
+        arrived(("s1", layer), r.sgk.at[layer, pl.ds(0, nk - 1)])
+        r.sgz[layer] = jnp.sum(r.sgk[layer], axis=0)
+        r.sgi[layer, i] = r.sgz[layer]
+
+        def one(j):
+            send(("s2", layer), r.sgz.at[layer], r.sgi.at[layer, i], at(lax.rem(i + j, ni), k))
+
+        loop(ni, one, 1)
+
+    def small_ready(layer):
+        arrived(("s2", layer), r.sgi.at[layer, pl.ds(0, ni - 1)])
+        r.out_s[layer, 0:32, :] = jnp.sum(r.sgi[layer], axis=0)
+        tiles = [r.mv[layer, :, LANES * tile : LANES * (tile + 1)] for tile in range(z.ct)]
+        mine = jnp.zeros((8, LANES), f32)
+        for part in range(nk):
+            mine = mine + jnp.where(k == part, cut(tiles, part * z.cl, z.cl), 0.0)
+        r.out_s[layer, 32:40, :] = mine
 
     for layer in reversed(range(layers)):
         above = layer + 1 if layer + 1 < layers else None
@@ -848,9 +884,6 @@
             r.gr["m"][layer, parts, z.fl : 2 * z.fl, :] = value
         if z.join_kind != "m":
             reduce_pair(layer, "m")
-        if above is not None:
-            reduce_along(above, "m")
-            reduce_along(above, "j")
 
         def token_back(t, carry, layer=layer):
             lines = pl.ds(t * z.step, z.step)
@@ -923,6 +956,15 @@
             r.msg[slot, tile : tile + 1, :] = first[:, lanes]
             r.msg[slot, z.ct + tile : z.ct + tile + 1, :] = second[:, lanes]
         exchange_start(slot)
+        if above is None:
+            swap_start(2)
+        else:
+            reduce_along(above, "m")
+            reduce_along(above, "j")
+        reduce_across(layer, "m")
+        reduce_across(layer, "j")
+        if above is not None:
+            small_across(above)
 
         rows_table = jnp.where(same_wide, rows_table, 0.0).reshape(z.high, z.tj, z.rb)
         rows_table = jnp.sum(rows_table, axis=1)
@@ -937,11 +979,6 @@
         r.mg[:, 16:32] = cols_table
         r.mg[0 : z.high, 32:33] = jnp.sum(rows_sum.reshape(z.high, z.tj, 1), axis=1)
         r.mg[:, 33:34] = jnp.sum(cols_sum.reshape(z.high, z.tj, 1), axis=0)
-        reduce_across(layer, "m")
-        reduce_across(layer, "j")
-        if above is not None:
-            spread_across(above, "m")
-            spread_across(above, "j")
 
         exchange_wait(slot)
         stats = jnp.sum(r.stats[slot], axis=0)
@@ -973,13 +1010,12 @@
         loop(z.own * (z.high // z.lines), conv_back)
 
         if layer == 0:
-
-            def take_gx(b, start, tile):
-                return r.gx[pl.ds(b * z.high + start, z.lines), :, LANES * tile : LANES * (tile + 1)]
-
-            pack(3, take_gx)
+            slices_of(r.gx, 3)
             swap_start(3)
             own_tile(3)
+        if above is not None:
+            spread_across(above, "m")
+            spread_across(above, "j")
 
         for tile in range(z.ct):
             lanes = slice(LANES * tile, LANES * (tile + 1))
@@ -1022,27 +1058,7 @@
             other = lax.rem(k + step, nk)
             send(("s1", layer), r.sgm.at[layer, other], r.sgk.at[layer, k], at(i, other))
 
-    def small_across(layer):
-        arrived(("s1", layer), r.sgk.at[layer, pl.ds(0, nk - 1)])
-        r.sgz[layer] = jnp.sum(r.sgk[layer], axis=0)
-        r.sgi[layer, i] = r.sgz[layer]
-
-        def one(j):
-            send(("s2", layer), r.sgz.at[layer], r.sgi.at[layer, i], at(lax.rem(i + j, ni), k))
-
-        loop(ni, one, 1)
-
-    def small_ready(layer):
-        arrived(("s2", layer), r.sgi.at[layer, pl.ds(0, ni - 1)])
-        r.out_s[layer, 0:32, :] = jnp.sum(r.sgi[layer], axis=0)
-        tiles = [r.mv[layer, :, LANES * tile : LANES * (tile + 1)] for tile in range(z.ct)]
-        mine = jnp.zeros((8, LANES), f32)
-        for part in range(nk):
-            mine = mine + jnp.where(k == part, cut(tiles, part * z.cl, z.cl), 0.0)
-        r.out_s[layer, 32:40, :] = mine
-
-    for layer in reversed(range(layers)):
-        small_across(layer)
+    small_across(0)
     reduce_along(0, "m")
     reduce_along(0, "j")
     for layer in range(1, layers):
@@ -1078,14 +1094,87 @@
 EVENTS = 80
 
 
+def finish(z, *refs):
+    count = 3 + len(z.parts)
+    sources, refs = refs[:count], refs[count:]
+    sem, copies, refs = refs[-1], refs[-1 - count : -1], refs[: -1 - count]
+    loads = [pltpu.make_async_copy(src, dst, sem.at[n]) for n, (src, dst) in enumerate(zip(sources, copies, strict=True))]
+    for load in loads:
+        load.start()
+    land_y, land_g, small = copies[:3]
+    fins = dict(zip(z.parts, copies[3:], strict=True))
+    mean_in, var_in = refs[:2]
+    (output, images_grad, conv_grad, bn_gain, bn_bias, rows_grad, rows_bias, cols_grad, cols_bias, join) = refs[2:12]
+    (join_bias, norm_gain, norm_bias, rising, bias_in, falling, bias_out, mean_out, var_out, tmp) = refs[12:]
+    for number, land, out in ((0, land_y, output), (1, land_g, images_grad)):
+        loads[number].wait()
+        for k in range(z.nk):
+
+            def group(first, tile, lines, tiles, land=land, k=k):
+                source = [land[k, tile + t].astype(f32) for t in range(tiles)]
+                for j in range(lines):
+                    m = first + j
+                    n = k * z.own + lax.div(m, z.high)
+                    tmp[lax.rem(m, z.high), pl.ds(n, z.wide, stride=z.group), :] = cut(source, j * z.cl, z.cl)[: z.wide]
+
+            line_groups(z, group)
+
+        def line(h, carry, out=out):
+            out[h] = tmp[h, :, 0 : z.cl].reshape(z.wide, z.group, z.cl).astype(out.dtype)
+            return carry
+
+        lax.fori_loop(0, z.high, line, 0)
+    for load in loads[2:]:
+        load.wait()
+    for layer in range(z.layers):
+        here = slice(layer, layer + 1)
+
+        def row(number, layer=layer):
+            return small[layer, number : number + 1, 0 : z.cl]
+
+        for tap in range(9):
+            conv_grad[tap // 3, tap % 3, here, :] = row(tap)
+        join_bias[here, :] = row(9)
+        norm_gain[here, :] = row(10)
+        norm_bias[here, :] = row(11)
+        bias_out[here, :] = row(12)
+        for tile in range(z.ftiles):
+            stop = min(z.fl, LANES * (tile + 1))
+            bias_in[here, LANES * tile : stop] = small[layer, 13 + tile : 14 + tile, 0 : stop - LANES * tile]
+        rows_grad[:, layer, :] = small[layer, 16 : 16 + z.high, 0 : z.high]
+        cols_grad[:, layer, :] = small[layer, 16 : 16 + z.wide, 16 : 16 + z.wide]
+        turned = small[layer, 16:32, :].T
+        rows_bias[here, :] = turned[32:33, 0 : z.high]
+        cols_bias[here, :] = turned[33:34, 0 : z.wide]
+        mean_out[here, :] = 0.9 * mean_in[here, :] + 0.1 * row(32)
+        var_out[here, :] = 0.9 * var_in[here, :] + (0.1 * z.cells / (z.cells - 1.0)) * row(33)
+        bn_gain[here, :] = row(35)
+        bn_bias[here, :] = row(36)
+        fin = fins["m"]
+        rising[layer] = fin[layer, 0 : z.fl, 0 : z.channels].astype(f32).T
+        falling[layer] = fin[layer, z.fl : 2 * z.fl, 0 : z.channels].astype(f32)
+        fin = fins[z.join_kind]
+        for branch in range(3):
+            start = z.join_row + branch * z.clp
+            join[layer, branch] = fin[layer, start : start + z.cl, 0 : z.channels].astype(f32)
+
+
+EVENTS = 80
+
+
 def on_device(ni, nk, *args):
+    first, second = (1, 2, 0, 3), (1, 0, 2)
+    args = list(args)
+    for number, order in ((0, first), (1, first), (18, first), (4, second), (6, second)):
+        args[number] = args[number].transpose(order)
     images, conv_kernel, weight_in = args[0], args[1], args[12]
     running_mean, running_var, cotangent = args[16:19]
     z = Sizes(ni, nk, images, conv_kernel, weight_in)
     inputs = (*args[:16], cotangent)
+    land = jax.ShapeDtypeStruct((nk, z.packed, z.tj, LANES), bf16)
     out_shape = (
-        jax.ShapeDtypeStruct((nk, z.own, z.high, z.tj, LANES), bf16),
-        jax.ShapeDtypeStruct((nk, z.own, z.high, z.tj, LANES), bf16),
+        land,
+        land,
         jax.ShapeDtypeStruct((z.layers, SMALL_ROWS, LANES), f32),
         *(jax.ShapeDtypeStruct((z.layers, ni * part, z.cp), bf16) for part in z.parts.values()),
     )
@@ -1093,7 +1182,7 @@
     shapes, groups = scratch_list(z)
     scratch = [pltpu.VMEM(shape, kind) for table in (shapes, *groups) for shape, kind in table.values()]
     scratch += [pltpu.SemaphoreType.DMA((EVENTS,)), pltpu.SemaphoreType.DMA((EVENTS,))]
-    out_y, out_g, out_s, *grads = pl.pallas_call(
+    moved = pl.pallas_call(
         functools.partial(whole, z),
         out_shape=out_shape,
         in_specs=[vmem] * len(inputs),
@@ -1103,38 +1192,45 @@
             collective_id=0, has_side_effects=True, vmem_limit_bytes=62 * 2**20
         ),
     )(*inputs)
-    grads = dict(zip(z.parts, grads, strict=True))
-    out_m, out_j = grads["m"], grads[z.join_kind][:, z.join_row :]
-    shape = (z.group, z.high, z.tj, LANES)
-    output = out_y.reshape(shape)[:, :, : z.wide, : z.cl]
-    images_grad = out_g.reshape(shape)[:, :, : z.wide, : z.cl].astype(f32)
-    rising = out_m[:, : z.fl, : z.channels].astype(f32).transpose(0, 2, 1)
-    falling = out_m[:, z.fl : 2 * z.fl, : z.channels].astype(f32)
-    join = out_j[:, : 3 * z.clp].reshape(z.layers, 3, z.clp, z.cp)[:, :, : z.cl, : z.channels].astype(f32)
-    kernel_grad = out_s[:, :9, : z.cl].reshape(z.layers, 3, 3, z.cl)
-    hidden_bias = out_s[:, 13 : 13 + z.ftiles, :].reshape(z.layers, -1)[:, : z.fl]
-    mean, var = out_s[:, 32, : z.cl], out_s[:, 33, : z.cl]
-    return (
-        output,
-        images_grad,
-        kernel_grad,
-        out_s[:, 35, : z.cl],
-        out_s[:, 36, : z.cl],
-        out_s[:, 16 : 16 + z.high, : z.high],
-        out_s[:, 16 : 16 + z.high, 32],
-        out_s[:, 16 : 16 + z.wide, 16 : 16 + z.wide],
-        out_s[:, 16 : 16 + z.wide, 33],
-        join,
-        out_s[:, 9, : z.cl],
-        out_s[:, 10, : z.cl],
-        out_s[:, 11, : z.cl],
-        rising,
-        hidden_bias,
-        falling,
-        out_s[:, 12, : z.cl],
-        0.9 * running_mean + 0.1 * mean,
-        0.9 * running_var + 0.1 * var * (z.cells / (z.cells - 1.0)),
-    )
+    lead = z.layers
+    tokens = (z.high, z.wide, z.group, z.cl)
+    sizes = [
+        (tokens, bf16),
+        (tokens, f32),
+        ((3, 3, lead, z.cl), f32),
+        ((lead, z.cl), f32),
+        ((lead, z.cl), f32),
+        ((z.high, lead, z.high), f32),
+        ((lead, z.high), f32),
+        ((z.wide, lead, z.wide), f32),
+        ((lead, z.wide), f32),
+        ((lead, 3, z.cl, z.channels), f32),
+        ((lead, z.cl), f32),
+        ((lead, z.cl), f32),
+        ((lead, z.cl), f32),
+        ((lead, z.channels, z.fl), f32),
+        ((lead, z.fl), f32),
+        ((lead, z.fl, z.channels), f32),
+        ((lead, z.cl), f32),
+        ((lead, z.cl), f32),
+        ((lead, z.cl), f32),
+    ]
+    results = pl.pallas_call(
+        functools.partial(finish, z),
+        out_shape=tuple(jax.ShapeDtypeStruct(*size) for size in sizes),
+        in_specs=[pl.BlockSpec(memory_space=pl.ANY)] * len(moved) + [vmem] * 2,
+        out_specs=(vmem,) * len(sizes),
+        scratch_shapes=[
+            pltpu.VMEM((z.high, z.wide * z.group, LANES), f32),
+            *(pltpu.VMEM(item.shape, item.dtype) for item in moved),
+            pltpu.SemaphoreType.DMA((len(moved),)),
+        ],
+        compiler_params=pltpu.CompilerParams(vmem_limit_bytes=62 * 2**20),
+    )(*moved, running_mean, running_var)
+    results = list(results)
+    for number, order in ((0, (2, 0, 1, 3)), (1, (2, 0, 1, 3)), (2, (2, 0, 1, 3)), (5, second), (7, second)):
+        results[number] = results[number].transpose(order)
+    return tuple(results)
 
 
 def solution(mesh):

time: 158 us -> 131 us (0.83)
  local copies, waits for them, and re-layouts: 11.7 us -> 0 us
  Pallas kernels: 139 us -> 130 us
  other arithmetic: 6.26 us -> 0 us
    pallas_call x1, Pallas kernels: 139 us -> 124 us  [on_device(): pl.pallas_call(functools.partial(whole, z), out_shape=out_shape, in_specs...]
    unnamed x31 -> x0, local copies, waits for them, and re-layouts: 9.42 us -> none
    pallas_call x0 -> x1, Pallas kernels: none -> 6.68 us  [on_device(): pl.pallas_call(functools.partial(finish, z), out_shape=tuple((jax.ShapeDt...]
    convert_element_type x3 -> x0, other arithmetic: 4.18 us -> none  [the longest x1 2.25 us: on_device(): falling = out_m[:, z.fl:2 * z.fl, :z.channels].astype(f32)]
where the time goes in v2:
time: 131 us
  Pallas kernels  130 us (99%)
    pallas_call x1, Pallas kernels, on_device(): pl.pallas_call(functools.partial(whole, z), out_shape=out_shape, in_specs...  124 us
    pallas_call x1, Pallas kernels, on_device(): pl.pallas_call(functools.partial(finish, z), out_shape=tuple((jax.ShapeDt...  6.68 us

profile of v2, /device:TPU:0, one launch (start us, length us, event | category | flops | bytes accessed | tf_op | source)
XLA Modules:
  0.0 131.0 jit_solution(16954995175853990079)
XLA Ops:
  0.7 123.5 %shard_map.330 = (bf16[4,18,16,128]{3,2,1,0:T(8,128)(2,1)}, bf16[4,18,16,128]{3,2,1,0:T(8,128)(2,1)}, f32[2,40,128]{2,1,0:T(8,128)}, bf16[2,640,384]{2,1,0:T(8,128)(2,1)}, bf16[2,256,384]{2,1,0:T(8,128)(2,1)}) custom-call(bf16[14,14,8,80]{3,2,1,0:T(8,128)(2,1)} %bitcast.11, bf16[3,3,2,80]{3,2,1,0:T(2,128)(2,1)} %bitcast.14, bf16[2,80]{1,0:T(2,128)(2,1)} %refs_2_.1, ...), custom_call_target="tpu_custom_call" | custom-call | tf_op jit(solution)/shard_map/pallas_call | solution.py:1185
  124.2 6.7 %shard_map.331 = (bf16[14,14,8,80]{3,2,1,0:T(8,128)(2,1)}, f32[14,14,8,80]{3,2,1,0:T(8,128)}, f32[3,3,2,80]{3,2,1,0:T(2,128)}, f32[2,80]{1,0:T(2,128)}, f32[2,80...) custom-call(bf16[4,18,16,128]{3,2,1,0:T(8,128)(2,1)} %get-tuple-elem, ...), custom_call_target="tpu_custom_call" | custom-call | tf_op jit(solution)/shard_map/pallas_call | solution.py:1218

commit v3 on v2

--- a/solution.py
+++ b/solution.py
@@ -191,6 +191,7 @@
         gb=((layer, z.nkg, z.own, z.rb, z.ft), bf16),
         gh=((z.own, z.rb, z.ft), bf16),
         o=((z.bh, z.tj, cp), f32),
+        y=((z.bh, z.tj, cp), f32),
         gx=((z.bh, z.tj, cp), f32),
         gob=((z.bh, z.tj, cp), bf16),
         gw=((z.bh, z.tj, cp), f32),
@@ -466,16 +467,18 @@
         arrived(("r5", layer, kind), r.fin[kind].at[layer, pl.ds(0, z.chips * rps(kind))])
         r.outs[kind][layer] = r.fin[kind][layer]
 
-    cleared = [r.tmp, r.xl, r.x, r.ga, r.par, r.pf, r.bi, r.mixs, r.mg, r.sg, r.bg, r.sgm]
-    for ref in cleared + list(r.gr.values()):
-        if len(ref.shape) > 3:
-
-            def clear(index, ref=ref):
-                ref[index] = jnp.zeros(ref.shape[1:], ref.dtype)
-
-            loop(ref.shape[0], clear)
-        else:
-            ref[...] = jnp.zeros(ref.shape, ref.dtype)
+    def clear(refs):
+        for ref in refs:
+            if len(ref.shape) > 3:
+
+                def clear_one(index, ref=ref):
+                    ref[index] = jnp.zeros(ref.shape[1:], ref.dtype)
+
+                loop(ref.shape[0], clear_one)
+            else:
+                ref[...] = jnp.zeros(ref.shape, ref.dtype)
+
+    clear([r.tmp, r.xl, r.par])
 
     tile_row = lax.broadcasted_iota(jnp.int32, (z.tj, LANES), 0)
     inside = tile_row < z.wide
@@ -577,6 +580,8 @@
     weights_along(0, "m")
     swap_start(0)
     own_tile(0)
+
+    clear([r.x, r.ga, r.pf, r.bi, r.mixs, r.mg, r.sg, r.bg, r.sgm, *r.gr.values()])
 
     select_row = lax.broadcasted_iota(jnp.int32, (z.rb, 16), 0)
     select_col = lax.broadcasted_iota(jnp.int32, (z.rb, 16), 1)
@@ -812,7 +817,7 @@
             if layer + 1 < layers:
                 r.x[layer + 1, b, 1 : z.high + 1] = value
             else:
-                r.o[lines] = value
+                r.y[lines] = value
 
         real_part = lax.broadcasted_iota(jnp.int32, (z.high, z.tj, z.cp), 1) < z.wide
         loop(z.own, mlp_part)
@@ -821,8 +826,6 @@
         take(r.cotangent, 1)
         swap_start(1)
         own_tile(1)
-    slices_of(r.o, 2)
-    own_tile(2)
     swap_wait(1)
     unpack(z, r.land.at[1], store_gx)
 
@@ -908,6 +911,42 @@
         r.sg[10:11, :] = jnp.sum(gain_sum, axis=0, keepdims=True)
         r.sg[11:12, :] = jnp.sum(bias_sum, axis=0, keepdims=True)
 
+        def mix_back(b, layer=layer):
+            lines = pl.ds(b * z.high, z.high)
+            low = r.gsb[lines].reshape(z.rb, z.cp)
+            total = r.gw[lines].reshape(z.rb, z.cp) + dot_nt(low, r.jf[layer, 0])
+            for which in range(2):
+                back = dot_nt(low, r.jf[layer, 1 + which]).astype(bf16)
+                r.gpq[which, b] = back
+                total = total + dot_nn(r.mix[layer, 2 * which + 1], back)
+            r.gu[lines] = total.reshape(z.high, z.tj, z.cp)
+
+        loop(z.own, mix_back)
+
+        inv_std = r.mv[layer, 2:3, :]
+        mean = r.mv[layer, 0:1, :]
+
+        def gate_back(t, carry, layer=layer, mean=mean, inv_std=inv_std):
+            lines = pl.ds(t * z.step, z.step)
+            value = r.gu[lines] * r.sz[layer, lines]
+            r.gz[lines] = value
+            centred = (r.a[layer, lines] - mean) * inv_std
+            return carry[0] + jnp.sum(value, axis=0), carry[1] + jnp.sum(value * centred, axis=0)
+
+        first, second = lax.fori_loop(0, blocks, gate_back, (zero, zero))
+        first = jnp.sum(first, axis=0, keepdims=True)
+        second = jnp.sum(second, axis=0, keepdims=True)
+        slot = layers + layer
+        for tile in range(z.ct):
+            lanes = slice(LANES * tile, LANES * (tile + 1))
+            r.msg[slot, tile : tile + 1, :] = first[:, lanes]
+            r.msg[slot, z.ct + tile : z.ct + tile + 1, :] = second[:, lanes]
+        exchange_start(slot)
+        if above is not None:
+            reduce_along(above, "m")
+            reduce_along(above, "j")
+        if z.join_kind != "m":
+            reduce_across(layer, "m")
         low_join = r.gsb[...].reshape(z.rows, z.cp)
         for branch in range(3):
             value = dot_tn(r.cat[layer, branch].reshape(z.rows, z.cp), low_join)
@@ -917,52 +956,27 @@
                     part * z.cl : (part + 1) * z.cl
                 ].astype(bf16)
         reduce_pair(layer, z.join_kind)
-
-        def mix_back(b, carry, layer=layer):
-            lines = pl.ds(b * z.high, z.high)
-            low = r.gsb[lines].reshape(z.rb, z.cp)
-            total = r.gw[lines].reshape(z.rb, z.cp) + dot_nt(low, r.jf[layer, 0])
-            tables, sums = [], []
-            for which in range(2):
-                value = dot_nt(low, r.jf[layer, 1 + which])
-                back = value.astype(bf16)
-                total = total + dot_nn(r.mix[layer, 2 * which + 1], back)
-                tables.append(carry[which] + dot_nt(back, r.cat[layer, 0, b]))
-                sums.append(carry[2 + which] + jnp.sum(value, axis=1, keepdims=True))
-            r.gu[lines] = total.reshape(z.high, z.tj, z.cp)
-            return (*tables, *sums)
+        if above is None:
+            slices_of(r.y, 2)
+            swap_start(2)
+            own_tile(2)
+
+        def tables_part(b, carry, layer=layer):
+            low = r.cat[layer, 0, b]
+            backs = [r.gpq[which, b] for which in range(2)]
+            return (
+                *(carry[which] + dot_nt(backs[which], low) for which in range(2)),
+                *(
+                    carry[2 + which] + jnp.sum(backs[which].astype(f32), axis=1, keepdims=True)
+                    for which in range(2)
+                ),
+            )
 
         square, column = jnp.zeros((z.rb, z.rb), f32), jnp.zeros((z.rb, 1), f32)
         rows_table, cols_table, rows_sum, cols_sum = lax.fori_loop(
-            0, z.own, mix_back, (square, square, column, column)
+            0, z.own, tables_part, (square, square, column, column)
         )
-
-        inv_std = r.mv[layer, 2:3, :]
-        mean = r.mv[layer, 0:1, :]
-
-        def gate_back(t, carry, layer=layer, mean=mean, inv_std=inv_std):
-            lines = pl.ds(t * z.step, z.step)
-            value = r.gu[lines] * r.sz[layer, lines]
-            r.gz[lines] = value
-            centred = (r.a[layer, lines] - mean) * inv_std
-            return carry[0] + jnp.sum(value, axis=0), carry[1] + jnp.sum(value * centred, axis=0)
-
-        first, second = lax.fori_loop(0, blocks, gate_back, (zero, zero))
-        first = jnp.sum(first, axis=0, keepdims=True)
-        second = jnp.sum(second, axis=0, keepdims=True)
-        slot = layers + layer
-        for tile in range(z.ct):
-            lanes = slice(LANES * tile, LANES * (tile + 1))
-            r.msg[slot, tile : tile + 1, :] = first[:, lanes]
-            r.msg[slot, z.ct + tile : z.ct + tile + 1, :] = second[:, lanes]
-        exchange_start(slot)
-        if above is None:
-            swap_start(2)
-        else:
-            reduce_along(above, "m")
-            reduce_along(above, "j")
-        reduce_across(layer, "m")
-        reduce_across(layer, "j")
+        reduce_across(layer, z.join_kind)
         if above is not None:
             small_across(above)
 
@@ -1013,9 +1027,6 @@
             slices_of(r.gx, 3)
             swap_start(3)
             own_tile(3)
-        if above is not None:
-            spread_across(above, "m")
-            spread_across(above, "j")
 
         for tile in range(z.ct):
             lanes = slice(LANES * tile, LANES * (tile + 1))
@@ -1058,23 +1069,26 @@
             other = lax.rem(k + step, nk)
             send(("s1", layer), r.sgm.at[layer, other], r.sgk.at[layer, k], at(i, other))
 
-    small_across(0)
+    for layer in range(1, layers):
+        spread_across(layer, "m")
+        spread_across(layer, "j")
     reduce_along(0, "m")
     reduce_along(0, "j")
+    small_across(0)
     for layer in range(1, layers):
         spread_pair(layer, "m")
         spread_pair(layer, "j")
+    swap_wait(2)
+    r.out_y[...] = r.land[2]
     spread_across(0, "m")
     spread_across(0, "j")
-    swap_wait(2)
-    r.out_y[...] = r.land[2]
     for layer in range(1, layers):
         small_ready(layer)
         spread_ready(layer, "m")
         spread_ready(layer, "j")
-    small_ready(0)
     swap_wait(3)
     r.out_g[...] = r.land[3]
+    small_ready(0)
     spread_pair(0, "m")
     spread_pair(0, "j")
     spread_ready(0, "m")

time: 131 us -> 123 us (0.939)
  Pallas kernels: 130 us -> 122 us
    pallas_call x1, Pallas kernels: 124 us -> 115 us  [on_device(): pl.pallas_call(functools.partial(whole, z), out_shape=out_shape, in_specs...]
where the time goes in v3:
time: 123 us
  Pallas kernels  122 us (99%)
    pallas_call x1, Pallas kernels, on_device(): pl.pallas_call(functools.partial(whole, z), out_shape=out_shape, in_specs...  115 us
    pallas_call x1, Pallas kernels, on_device(): pl.pallas_call(functools.partial(finish, z), out_shape=tuple((jax.ShapeDt...  6.68 us

profile of v3, /device:TPU:0, one launch (start us, length us, event | category | flops | bytes accessed | tf_op | source)
XLA Modules:
  0.0 122.6 jit_solution(6032464486819141309)
XLA Ops:
  0.7 115.1 %shard_map.330 = (bf16[4,18,16,128]{3,2,1,0:T(8,128)(2,1)}, bf16[4,18,16,128]{3,2,1,0:T(8,128)(2,1)}, f32[2,40,128]{2,1,0:T(8,128)}, bf16[2,640,384]{2,1,0:T(8,128)(2,1)}, bf16[2,256,384]{2,1,0:T(8,128)(2,1)}) custom-call(bf16[14,14,8,80]{3,2,1,0:T(8,128)(2,1)} %bitcast.11, bf16[3,3,2,80]{3,2,1,0:T(2,128)(2,1)} %bitcast.14, bf16[2,80]{1,0:T(2,128)(2,1)} %refs_2_.1, ...), custom_call_target="tpu_custom_call" | custom-call | tf_op jit(solution)/shard_map/pallas_call | solution.py:1199
  115.8 6.7 %shard_map.331 = (bf16[14,14,8,80]{3,2,1,0:T(8,128)(2,1)}, f32[14,14,8,80]{3,2,1,0:T(8,128)}, f32[3,3,2,80]{3,2,1,0:T(2,128)}, f32[2,80]{1,0:T(2,128)}, f32[2,80...) custom-call(bf16[4,18,16,128]{3,2,1,0:T(8,128)(2,1)} %get-tuple-elem, ...), custom_call_target="tpu_custom_call" | custom-call | tf_op jit(solution)/shard_map/pallas_call | solution.py:1232

commit v4 on v3

--- a/solution.py
+++ b/solution.py
@@ -163,6 +163,8 @@
     layer, rows, cp = z.layers, z.rows, z.cp
     shapes = dict(
         tmp=((z.high, z.wide * z.group, LANES), f32),
+        fy=((z.high, z.wide, z.group, z.cl), bf16),
+        fg=((z.high, z.wide, z.group, z.cl), f32),
         xl=((z.group, z.high + 2, z.tj, LANES), f32),
         al=((z.group, z.high, z.tj, LANES), f32),
         stage=((4, z.nk) + tile, bf16),
@@ -241,7 +243,7 @@
             getattr(table, name)[kind] = ref
         refs = refs[len(group) :]
     r.wt, r.gr, r.r1, r.r2, r.r3, r.fin = table.wt, table.gr, table.r1, table.r2, table.r3, table.fin
-    ssem, rsem = refs
+    ssem, rsem, osem = refs
     ni, nk, nd, layers = z.ni, z.nk, z.nd, z.layers
     i = lax.axis_index("img")
     k = lax.axis_index("ch")
@@ -250,6 +252,7 @@
     partner = i + 1 - 2 * core
     events = {}
     sends = []
+    stores = []
 
     def at(image_index, channel_index):
         return {"img": image_index, "ch": channel_index}
@@ -279,6 +282,11 @@
             device_id=at(partner, k),
             device_id_type=MESH,
         ).wait_recv()
+
+    def store(src, dst):
+        copy = pltpu.make_async_copy(src, dst, osem.at[len(stores)])
+        stores.append(copy)
+        copy.start()
 
     def loop(count, body, start=0):
         def run(index, carry):
@@ -465,7 +473,7 @@
     @once
     def spread_ready(layer, kind):
         arrived(("r5", layer, kind), r.fin[kind].at[layer, pl.ds(0, z.chips * rps(kind))])
-        r.outs[kind][layer] = r.fin[kind][layer]
+        store(r.fin[kind].at[layer], r.outs[kind].at[layer])
 
     def clear(refs):
         for ref in refs:
@@ -866,19 +874,11 @@
             falling = r.wt["m"][layer, parts, z.fl : 2 * z.fl, :].reshape(z.ft, z.cp)
             rising = r.wt["m"][layer, parts, 0 : z.fl, :].reshape(z.ft, z.cp)
 
-            def back_part(b, carry, layer=layer, block=block, falling=falling, rising=rising):
-                lines = pl.ds(b * z.high, z.high)
-                low = r.gob[lines].reshape(z.rb, z.cp)
-                value = dot_nt(low, falling) * r.hs[layer, block, b]
-                low = value.astype(bf16)
-                r.gh[b] = low
-                term = dot_nn(low, rising).reshape(z.high, z.tj, z.cp)
-                r.o[lines] = term if block == 0 else r.o[lines] + term
-                return carry + jnp.sum(value, axis=0, keepdims=True)
-
-            total = lax.fori_loop(0, z.own, back_part, jnp.zeros((1, z.ft), f32))
-            r.bg[0:1, block * z.ft : (block + 1) * z.ft] = total
-            low_hidden = r.gh[...].reshape(z.rows, z.ft)
+            value = dot_nt(low_out, falling) * r.hs[layer, block].reshape(z.rows, z.ft)
+            r.bg[0:1, block * z.ft : (block + 1) * z.ft] = jnp.sum(value, axis=0, keepdims=True)
+            low_hidden = value.astype(bf16)
+            term = dot_nn(low_hidden, rising).reshape(z.bh, z.tj, z.cp)
+            r.o[...] = term if block == 0 else r.o[...] + term
             low_in = r.yb[layer].reshape(z.rows, z.cp)
             value = dot_tn(low_hidden, low_in).astype(bf16).reshape(z.kg, z.fl, z.cp)
             r.gr["m"][layer, parts, 0 : z.fl, :] = value
@@ -1069,6 +1069,9 @@
             other = lax.rem(k + step, nk)
             send(("s1", layer), r.sgm.at[layer, other], r.sgk.at[layer, k], at(i, other))
 
+    swap_wait(2)
+    deliver(z, r.land.at[2], r.tmp, r.fy)
+    store(r.fy, r.out_y)
     for layer in range(1, layers):
         spread_across(layer, "m")
         spread_across(layer, "j")
@@ -1078,22 +1081,23 @@
     for layer in range(1, layers):
         spread_pair(layer, "m")
         spread_pair(layer, "j")
-    swap_wait(2)
-    r.out_y[...] = r.land[2]
+    swap_wait(3)
+    deliver(z, r.land.at[3], r.tmp, r.fg)
+    store(r.fg, r.out_g)
     spread_across(0, "m")
     spread_across(0, "j")
     for layer in range(1, layers):
         small_ready(layer)
         spread_ready(layer, "m")
         spread_ready(layer, "j")
-    swap_wait(3)
-    r.out_g[...] = r.land[3]
     small_ready(0)
     spread_pair(0, "m")
     spread_pair(0, "j")
     spread_ready(0, "m")
     spread_ready(0, "j")
 
+    for copy in stores:
+        copy.wait()
     for number, ref in sends:
         pltpu.make_async_remote_copy(
             src_ref=ref,
@@ -1108,36 +1112,38 @@
 EVENTS = 80
 
 
+def deliver(z, land, tmp, out):
+    for k in range(z.nk):
+
+        def group(first, tile, lines, tiles, k=k):
+            source = [land[k, tile + t].astype(f32) for t in range(tiles)]
+            for j in range(lines):
+                m = first + j
+                n = k * z.own + lax.div(m, z.high)
+                tmp[lax.rem(m, z.high), pl.ds(n, z.wide, stride=z.group), :] = cut(source, j * z.cl, z.cl)[: z.wide]
+
+        line_groups(z, group)
+
+    def line(h, carry):
+        out[h] = tmp[h, :, 0 : z.cl].reshape(z.wide, z.group, z.cl).astype(out.dtype)
+        return carry
+
+    lax.fori_loop(0, z.high, line, 0)
+
+
 def finish(z, *refs):
     count = 3 + len(z.parts)
     sources, refs = refs[:count], refs[count:]
-    sem, copies, refs = refs[-1], refs[-1 - count : -1], refs[: -1 - count]
+    sem, copies, refs = refs[-1], refs[1 - count : -1], refs[: 1 - count]
+    copies = (refs[2], refs[3], *copies)
     loads = [pltpu.make_async_copy(src, dst, sem.at[n]) for n, (src, dst) in enumerate(zip(sources, copies, strict=True))]
     for load in loads:
         load.start()
-    land_y, land_g, small = copies[:3]
+    small = copies[2]
     fins = dict(zip(z.parts, copies[3:], strict=True))
     mean_in, var_in = refs[:2]
-    (output, images_grad, conv_grad, bn_gain, bn_bias, rows_grad, rows_bias, cols_grad, cols_bias, join) = refs[2:12]
-    (join_bias, norm_gain, norm_bias, rising, bias_in, falling, bias_out, mean_out, var_out, tmp) = refs[12:]
-    for number, land, out in ((0, land_y, output), (1, land_g, images_grad)):
-        loads[number].wait()
-        for k in range(z.nk):
-
-            def group(first, tile, lines, tiles, land=land, k=k):
-                source = [land[k, tile + t].astype(f32) for t in range(tiles)]
-                for j in range(lines):
-                    m = first + j
-                    n = k * z.own + lax.div(m, z.high)
-                    tmp[lax.rem(m, z.high), pl.ds(n, z.wide, stride=z.group), :] = cut(source, j * z.cl, z.cl)[: z.wide]
-
-            line_groups(z, group)
-
-        def line(h, carry, out=out):
-            out[h] = tmp[h, :, 0 : z.cl].reshape(z.wide, z.group, z.cl).astype(out.dtype)
-            return carry
-
-        lax.fori_loop(0, z.high, line, 0)
+    (conv_grad, bn_gain, bn_bias, rows_grad, rows_bias, cols_grad, cols_bias, join) = refs[4:12]
+    (join_bias, norm_gain, norm_bias, rising, bias_in, falling, bias_out, mean_out, var_out) = refs[12:]
     for load in loads[2:]:
         load.wait()
     for layer in range(z.layers):
@@ -1171,6 +1177,8 @@
         for branch in range(3):
             start = z.join_row + branch * z.clp
             join[layer, branch] = fin[layer, start : start + z.cl, 0 : z.channels].astype(f32)
+    for load in loads[:2]:
+        load.wait()
 
 
 EVENTS = 80
@@ -1185,29 +1193,28 @@
     running_mean, running_var, cotangent = args[16:19]
     z = Sizes(ni, nk, images, conv_kernel, weight_in)
     inputs = (*args[:16], cotangent)
-    land = jax.ShapeDtypeStruct((nk, z.packed, z.tj, LANES), bf16)
+    tokens = (z.high, z.wide, z.group, z.cl)
     out_shape = (
-        land,
-        land,
+        jax.ShapeDtypeStruct(tokens, bf16),
+        jax.ShapeDtypeStruct(tokens, f32),
         jax.ShapeDtypeStruct((z.layers, SMALL_ROWS, LANES), f32),
         *(jax.ShapeDtypeStruct((z.layers, ni * part, z.cp), bf16) for part in z.parts.values()),
     )
-    vmem = pl.BlockSpec(memory_space=pltpu.VMEM)
+    vmem, anywhere = pl.BlockSpec(memory_space=pltpu.VMEM), pl.BlockSpec(memory_space=pl.ANY)
     shapes, groups = scratch_list(z)
     scratch = [pltpu.VMEM(shape, kind) for table in (shapes, *groups) for shape, kind in table.values()]
-    scratch += [pltpu.SemaphoreType.DMA((EVENTS,)), pltpu.SemaphoreType.DMA((EVENTS,))]
+    scratch += [pltpu.SemaphoreType.DMA((EVENTS,)), pltpu.SemaphoreType.DMA((EVENTS,)), pltpu.SemaphoreType.DMA((16,))]
     moved = pl.pallas_call(
         functools.partial(whole, z),
         out_shape=out_shape,
         in_specs=[vmem] * len(inputs),
-        out_specs=(vmem,) * len(out_shape),
+        out_specs=tuple(vmem if number == 2 else anywhere for number in range(len(out_shape))),
         scratch_shapes=scratch,
         compiler_params=pltpu.CompilerParams(
             collective_id=0, has_side_effects=True, vmem_limit_bytes=62 * 2**20
         ),
     )(*inputs)
     lead = z.layers
-    tokens = (z.high, z.wide, z.group, z.cl)
     sizes = [
         (tokens, bf16),
         (tokens, f32),
@@ -1232,11 +1239,10 @@
     results = pl.pallas_call(
         functools.partial(finish, z),
         out_shape=tuple(jax.ShapeDtypeStruct(*size) for size in sizes),
-        in_specs=[pl.BlockSpec(memory_space=pl.ANY)] * len(moved) + [vmem] * 2,
+        in_specs=[anywhere] * len(moved) + [vmem] * 2,
         out_specs=(vmem,) * len(sizes),
         scratch_shapes=[
-            pltpu.VMEM((z.high, z.wide * z.group, LANES), f32),
-            *(pltpu.VMEM(item.shape, item.dtype) for item in moved),
+            *(pltpu.VMEM(item.shape, item.dtype) for item in moved[2:]),
             pltpu.SemaphoreType.DMA((len(moved),)),
         ],
         compiler_params=pltpu.CompilerParams(vmem_limit_bytes=62 * 2**20),

time: 123 us -> 122 us (level); the launches traced: 123 us -> 120 us
  Pallas kernels: 122 us -> 120 us
    pallas_call x1, Pallas kernels: 6.68 us -> 4.76 us  [on_device(): pl.pallas_call(functools.partial(finish, z), out_shape=tuple((jax.ShapeDt...]
where the time goes in v4:
time: 122 us; the launch traced here: 120 us
  Pallas kernels  120 us (98%)
    pallas_call x1, Pallas kernels, on_device(): pl.pallas_call(functools.partial(whole, z), out_shape=out_shape, in_specs...  115 us
    pallas_call x1, Pallas kernels, on_device(): pl.pallas_call(functools.partial(finish, z), out_shape=tuple((jax.ShapeDt...  4.76 us

profile of v4, /device:TPU:0, one launch (start us, length us, event | category | flops | bytes accessed | tf_op | source)
XLA Modules:
  0.0 120.4 jit_solution(13090936644975724714)
XLA Ops:
  0.7 114.8 %shard_map.330 = (bf16[14,14,8,80]{3,2,1,0:T(8,128)(2,1)}, f32[14,14,8,80]{3,2,1,0:T(8,128)}, f32[2,40,128]{2,1,0:T(8,128)}, bf16[2,640,384]{2,1,0:T(8,128)(2,1)}, bf16[2,256,384]{2,1,0:T(8,128)(2,1)}) custom-call(bf16[14,14,8,80]{3,2,1,0:T(8,128)(2,1)} %bitcast.11, bf16[3,3,2,80]{3,2,1,0:T(2,128)(2,1)} %bitcast.14, bf16[2,80]{1,0:T(2,128)(2,1)} %refs_2_.1, ...), custom_call_target="tpu_custom_call" | custom-call | tf_op jit(solution)/shard_map/pallas_call | solution.py:1207
  115.4 4.8 %shard_map.331 = (bf16[14,14,8,80]{3,2,1,0:T(8,128)(2,1)}, f32[14,14,8,80]{3,2,1,0:T(8,128)}, f32[3,3,2,80]{3,2,1,0:T(2,128)}, f32[2,80]{1,0:T(2,128)}, f32[2,80...) custom-call(bf16[14,14,8,80]{3,2,1,0:T(8,128)(2,1)} %get-tuple-eleme, ...), custom_call_target="tpu_custom_call" | custom-call | tf_op jit(solution)/shard_map/pallas_call | solution.py:1239

commit v5 on v4

--- a/solution.py
+++ b/solution.py
@@ -162,7 +162,7 @@
     tile = (z.packed, z.tj, LANES)
     layer, rows, cp = z.layers, z.rows, z.cp
     shapes = dict(
-        tmp=((z.high, z.wide * z.group, LANES), f32),
+        tmp=((z.high, z.tj * z.group, LANES), f32),
         fy=((z.high, z.wide, z.group, z.cl), bf16),
         fg=((z.high, z.wide, z.group, z.cl), f32),
         xl=((z.group, z.high + 2, z.tj, LANES), f32),
@@ -493,7 +493,7 @@
 
     def take(ref, slot):
         def line(h):
-            r.tmp[h, :, 0 : z.cl] = ref[h].astype(f32).reshape(z.wide * z.group, z.cl)
+            r.tmp[h, 0 : z.wide * z.group, 0 : z.cl] = ref[h].astype(f32).reshape(z.wide * z.group, z.cl)
             for n in range(z.group):
                 r.xl[n, h + 1, 0 : z.wide, :] = r.tmp[h, pl.ds(n, z.wide, stride=z.group), :]
 
@@ -1125,7 +1125,7 @@
         line_groups(z, group)
 
     def line(h, carry):
-        out[h] = tmp[h, :, 0 : z.cl].reshape(z.wide, z.group, z.cl).astype(out.dtype)
+        out[h] = tmp[h, 0 : z.wide * z.group, 0 : z.cl].reshape(z.wide, z.group, z.cl).astype(out.dtype)
         return carry
 
     lax.fori_loop(0, z.high, line, 0)

time: 122 us -> 122 us (level)
  no operation moved by 1% of the time
where the time goes in v5:
time: 122 us; the launch traced here: 120 us
  Pallas kernels  120 us (98%)
    pallas_call x1, Pallas kernels, on_device(): pl.pallas_call(functools.partial(whole, z), out_shape=out_shape, in_specs...  115 us
    pallas_call x1, Pallas kernels, on_device(): pl.pallas_call(functools.partial(finish, z), out_shape=tuple((jax.ShapeDt...  4.76 us

profile of v5, /device:TPU:0, one launch (start us, length us, event | category | flops | bytes accessed | tf_op | source)
XLA Modules:
  0.0 120.4 jit_solution(8226012236618852005)
XLA Ops:
  0.7 114.8 %shard_map.330 = (bf16[14,14,8,80]{3,2,1,0:T(8,128)(2,1)}, f32[14,14,8,80]{3,2,1,0:T(8,128)}, f32[2,40,128]{2,1,0:T(8,128)}, bf16[2,640,384]{2,1,0:T(8,128)(2,1)}, bf16[2,256,384]{2,1,0:T(8,128)(2,1)}) custom-call(bf16[14,14,8,80]{3,2,1,0:T(8,128)(2,1)} %bitcast.11, bf16[3,3,2,80]{3,2,1,0:T(2,128)(2,1)} %bitcast.14, bf16[2,80]{1,0:T(2,128)(2,1)} %refs_2_.1, ...), custom_call_target="tpu_custom_call" | custom-call | tf_op jit(solution)/shard_map/pallas_call | solution.py:1207
  115.4 4.8 %shard_map.331 = (bf16[14,14,8,80]{3,2,1,0:T(8,128)(2,1)}, f32[14,14,8,80]{3,2,1,0:T(8,128)}, f32[3,3,2,80]{3,2,1,0:T(2,128)}, f32[2,80]{1,0:T(2,128)}, f32[2,80...) custom-call(bf16[14,14,8,80]{3,2,1,0:T(8,128)(2,1)} %get-tuple-eleme, ...), custom_call_target="tpu_custom_call" | custom-call | tf_op jit(solution)/shard_map/pallas_call | solution.py:1239
